TPU v7x, 32 devices: a whole 2x2x4 slice. The times are simulated.
32 devices in a mesh: dp: 2 (over core), seq: 4 (over z), tensor: 4 (over y, x).
Axes of the slice: x: 2, y: 2, z: 4, core: 2. Of those that a mesh axis runs over, the one named last changes fastest.
Arguments:
- query: bfloat16 [2, 1024, 2048], P('dp', 'seq', 'tensor'), may hold values from -1.75 to 1.75
- key_rows: bfloat16 [2, 1024, 2048], P('dp', 'seq', 'tensor'), may hold values from -1.75 to 1.75
- value: bfloat16 [2, 1024, 2048], P('dp', 'seq', 'tensor'), may hold values from -40 to 40
- gain: float32 [2048], P('tensor'), may hold values from 0.25 to 1.75
- grad_out: bfloat16 [2, 1024, 2048], P('dp', 'seq', 'tensor'), may hold values from -16 to 16
- start_offset: int32 [2, 16], P('dp', 'seq'), may hold values from 0 to 64, as said below
Outputs:
- attn_out: bfloat16 [2, 1024, 2048], P('dp', 'seq', 'tensor')
- grad_query: bfloat16 [2, 1024, 2048], P('dp', 'seq', 'tensor')
- grad_key: bfloat16 [2, 1024, 2048], P('dp', 'seq', 'tensor')
- grad_value: bfloat16 [2, 1024, 2048], P('dp', 'seq', 'tensor')
- grad_gain: float32 [2048], P('tensor')
Inputs may be any that keep to these rules, and one draw needn't show every extreme that they name: `start_offset`: the position within its block of 64 positions at which a document starts; 64 when none starts in the block; every sequence begins a document at its first position.
All inputs are finite; a program needn't handle non-finite values.
Results may differ from a plain program's by a relative error of at most 0.0058.
Values sent between devices are 32-bit elements; how exact they have to be, the bound alone decides.
A program may use at most 64 MiB of HBM per device.

v0:
```python
import jax
import jax.numpy as jnp
from jax import lax
from jax.sharding import PartitionSpec as P

DH = 128
BLK = 64
CH = 2048


eps_value = 1e-05


def carried_in(part, axis, combine, identity, reverse):
    count = lax.axis_size(axis)
    place = lax.axis_index(axis)
    ahead = count - 1 - place if reverse else place
    gathered = jax.tree.map(lambda a: lax.all_gather(a, axis), part)
    state = jax.tree.map(lambda a, e: jnp.zeros_like(a) + jnp.asarray(e, a.dtype), part, identity)

    def one(turn, state):
        source = count - 1 - turn if reverse else turn
        return combine(
            state, jax.tree.map(lambda a: lax.dynamic_index_in_dim(a, source, 0, False), gathered)
        )

    return lax.fori_loop(0, ahead, one, state)


def segment_rows(offsets, length_dev):
    positions = jnp.arange(length_dev, dtype=jnp.int32)
    block_starts = jnp.arange(offsets.shape[0], dtype=jnp.int32) * BLK + offsets
    present = offsets < BLK
    covered = (block_starts[None, :] <= positions[:, None]) & present[None, :]
    labels = jnp.sum(covered.astype(jnp.int32), axis=1)
    allowed = (labels[:, None] == labels[None, :]) & (positions[None, :] <= positions[:, None])
    starts = jnp.sum(present.astype(jnp.int32))
    return (labels, starts, allowed)


def joined(earlier, later):
    return (
        jnp.where(later[1] > 0, later[0], earlier[0] + later[0]),
        jnp.maximum(earlier[1], later[1]),
    )


def shards(query, key_rows, value, gain, grad_out, start_offset):
    length_dev = query.shape[1]
    width_local = query.shape[2]
    heads_local = width_local // DH
    query_heads = query[0].reshape(length_dev, heads_local, DH)
    key_heads = key_rows[0].reshape(length_dev, heads_local, DH)
    value_heads = value[0].reshape(length_dev, heads_local, DH)
    labels, starts, allowed = segment_rows(start_offset[0], length_dev)
    head_mask = (labels == 0)[:, None, None]
    tail_mask = (labels == starts)[:, None, None]
    reset = (starts > 0).astype(jnp.int32)
    scores = jnp.einsum("thd,shd->hts", query_heads, key_heads, preferred_element_type=jnp.float32)
    weights = jnp.where(allowed[None], scores, 0.0).astype(jnp.bfloat16)
    local_out = jnp.einsum("hts,shd->thd", weights, value_heads, preferred_element_type=jnp.float32)
    tail_keys = jnp.where(tail_mask, key_heads, jnp.zeros_like(key_heads))
    tail_values = jnp.where(tail_mask, value_heads, jnp.zeros_like(value_heads))
    tail_state = jnp.einsum(
        "shi,shj->hij", tail_keys, value_heads, preferred_element_type=jnp.float32
    )
    zero_state = jnp.zeros_like(tail_state)
    incoming = carried_in((tail_state, reset), "seq", joined, (zero_state, jnp.int32(0)), False)[0]
    carried = incoming.astype(jnp.bfloat16)
    head_query = jnp.where(head_mask, query_heads, jnp.zeros_like(query_heads))
    carried_out = jnp.einsum(
        "thi,hij->thj", head_query, carried, preferred_element_type=jnp.float32
    )
    attended = (local_out + carried_out).reshape(length_dev, width_local)
    upstream = grad_out[0].astype(jnp.float32)
    scaled = gain[None, :] * upstream
    square_local = jnp.sum(attended * attended, axis=1)
    square_total, raw_total = lax.psum((square_local, jnp.sum(scaled * attended, axis=1)), "tensor")
    inverse = lax.rsqrt(square_total / CH + eps_value)
    normed = attended * inverse[:, None]
    product_total = raw_total * inverse
    output = (gain[None, :] * normed).astype(jnp.bfloat16)
    grad_pre = (inverse[:, None] * (scaled - normed * (product_total / CH)[:, None])).astype(
        jnp.bfloat16
    )
    gain_local = jnp.sum(upstream * normed, axis=0)
    grad_gain = lax.psum(gain_local, ("dp", "seq"))
    grad_heads = grad_pre.reshape(length_dev, heads_local, DH)
    grad_state = jnp.einsum(
        "thi,thj->hij", head_query, grad_heads, preferred_element_type=jnp.float32
    )
    later = carried_in((grad_state, reset), "seq", joined, (zero_state, jnp.int32(0)), True)[0]
    later_half = later.astype(jnp.bfloat16)
    grad_scores = jnp.einsum(
        "thd,shd->hts", grad_heads, value_heads, preferred_element_type=jnp.float32
    )
    grad_weights = jnp.where(allowed[None], grad_scores, 0.0).astype(jnp.bfloat16)
    head_grad = jnp.where(head_mask, grad_heads, jnp.zeros_like(grad_heads))
    grad_query = jnp.einsum(
        "hts,shd->thd", grad_weights, key_heads, preferred_element_type=jnp.float32
    ) + jnp.einsum("thj,hij->thi", head_grad, carried, preferred_element_type=jnp.float32)
    grad_key = jnp.einsum(
        "hts,thd->shd", grad_weights, query_heads, preferred_element_type=jnp.float32
    ) + jnp.einsum("shj,hij->shi", tail_values, later_half, preferred_element_type=jnp.float32)
    grad_value = jnp.einsum(
        "hts,thd->shd", weights, grad_heads, preferred_element_type=jnp.float32
    ) + jnp.einsum("shi,hij->shj", tail_keys, later_half, preferred_element_type=jnp.float32)
    shape_dev = (1, length_dev, width_local)
    return (
        output.reshape(shape_dev),
        grad_query.reshape(shape_dev).astype(jnp.bfloat16),
        grad_key.reshape(shape_dev).astype(jnp.bfloat16),
        grad_value.reshape(shape_dev).astype(jnp.bfloat16),
        grad_gain,
    )


def solution(mesh):
    return jax.shard_map(
        shards,
        mesh=mesh,
        in_specs=(
            P("dp", "seq", "tensor"),
            P("dp", "seq", "tensor"),
            P("dp", "seq", "tensor"),
            P("tensor"),
            P("dp", "seq", "tensor"),
            P("dp", "seq"),
        ),
        out_specs=(
            P("dp", "seq", "tensor"),
            P("dp", "seq", "tensor"),
            P("dp", "seq", "tensor"),
            P("dp", "seq", "tensor"),
            P("tensor"),
        ),
        check_vma=False,
    )
```

profile of v0, /device:TPU:0, one launch (start us, length us, event | category | flops | bytes accessed | tf_op | source)
XLA Modules:
  0.0 103.5 jit_solution(14556935447806349043)
XLA Ops:
  7.2 0.7 compare_bitcast_fusion
  7.9 0.6 fusion.27
  8.5 1.1 %copy.54 = bf16[1,256,512]{1,2,0:T(8,128)(2,1)S(1)} copy(bf16[1,256,512]{2,1,0:T(8,128)(2,1)} %param.11) | data formatting | bytes 524288 | tf_op args[1]
  9.9 0.6 broadcast_compare_fusion.1
  10.6 0.9 fusion.14
  12.3 0.6 copy-done.6
  12.9 0.6 dynamic-slice
  13.5 0.8 dynamic-update-slice
  14.3 9.9 %all-reduce = s32[4]{0:T(128)S(1)} all-reduce(s32[4]{0:T(128)S(1)} %dynamic-update-slice), channel_id=1, replica_groups=mesh['dp'=2,'seq'=4,'tensor'=4] {'seq'}, use_global_device_ids=true, to_apply=%add | all-reduce | flops 4 | bytes 32
  24.3 0.8 copy-done
  25.3 0.3 fusion
  26.0 16.4 %all-gather.5.cloned.1.call-done = f32[16,128,128]{2,1,0:T(8,128)} async-done(((f32[4,128,128]{2,1,0:T(8,128)}), f32[16,128,128]{2,1,0:T(8,128)}) %all-gather.5.cloned.1.call-update) | async-done | bytes 1048592 | tf_op jit(solution)/shard_map/all_gather | solution.py:18
  42.4 0.7 copy-done.4
  43.1 0.3 multiply_reduce_fusion
  43.4 9.9 %all-reduce.1 = (f32[256]{0:T(256)S(1)}, f32[256]{0:T(256)S(1)}) all-reduce(f32[256]{0:T(256)S(1)} %get-tuple-element.151, f32[256]{0:T(256)S(1)} %get-tuple-element.150), channel_id=1, replica_groups=mesh['dp'=2,'seq'=4,'tensor'=4] {'tensor'}, use_global_device_ids=true, to_apply=%region_5.6 | all-reduce | flops 512 | bytes 4096 | tf_op jit(solution)/shard_map/psum | solution.py:78
  53.5 0.9 fusion.15
  54.4 0.3 fusion.1
  55.3 0.8 copy.71
  56.4 1.0 copy.70
  57.4 1.2 %fusion.8 = f32[512]{0:T(512)S(1)} fusion(f32[256,512]{1,0:T(8,128)} %copy.70, f32[256]{0:T(256)S(1)} %get-tuple-element.175, bf16[1,256,512]{2,1,0:T(8,128)(2,1)S(1)} %copy-done.1), kind=kLoop, calls=%fused_computation.20 | loop fusion | flops 523776 | bytes 789504 | tf_op jit(solution)/shard_map/reduce_sum | solution.py:86
  58.6 21.6 %psum.23 = f32[512]{0:T(512)} all-reduce(f32[512]{0:T(512)S(1)} %fusion.8), channel_id=1, replica_groups=mesh['dp'=2,'seq'=4,'tensor'=4] {'dp','seq'}, use_global_device_ids=true, to_apply=%region_11.12 | all-reduce | flops 512 | bytes 4096 | tf_op jit(solution)/shard_map/psum | solution.py:87
  80.2 0.8 multiply_convert_fusion.1
  81.4 6.1 %all-gather.7.cloned.1.call-done = f32[16,128,128]{2,1,0:T(8,128)} async-done(((f32[4,128,128]{2,1,0:T(8,128)}), f32[16,128,128]{2,1,0:T(8,128)}) %all-gather.7.cloned.1.call-update) | async-done | bytes 1048592 | tf_op jit(solution)/shard_map/all_gather | solution.py:18
  87.5 7.0 %while.27 = (s32[]{:T(128)}, f32[4,128,128]{2,1,0:T(8,128)S(1)}, s32[]{:T(128)}, s32[4]{0:T(128)S(1)}, f32[4,4,128,128]{3,2,1,0:T(8,128)}, /*index=5*/s32[]{:T(128)}, s32[]{:T(128)}, s32[]{:T(128)}, s32[]{:T(128)}, s32[1]{0:T(128)}) while((s32[]{:T(128)}, f32[4,128,128]{2,1,0:T(8,128)S(1)}, s32[]{:T(128)}, s32[4]{0:T(128)S(1)}, ...), condition=%wide.region_9.10_spmd, body=%wide.region_8.9_spmd.sunk | while | flops 131079 | bytes 786613 | solution.py:27
  87.6 0.6 dynamic_slice.35
  88.8 1.1 %add_select_fusion.5 = f32[4,128,128]{2,1,0:T(8,128)S(1)} fusion(f32[4,128,128]{2,1,0:T(8,128)S(1)} %get-tuple-element.283, f32[4,4,128,128]{3,2,1,0:T(8,128)} %get-tuple-element.296, s32[]{:T(128)S(6)} %select_n.100, pred[]{:T(512)} %bitcast.73), kind=kLoop, calls=%fused_computation.1.clone.1 | loop fusion | flops 131072 | bytes 786437 | tf_op jit(solution)/shard_map/while/body/jit(_where)/select_n | solution.py:43
  89.9 0.6 dynamic_slice.35
  91.1 1.1 %add_select_fusion.5 = f32[4,128,128]{2,1,0:T(8,128)S(1)} fusion(f32[4,128,128]{2,1,0:T(8,128)S(1)} %get-tuple-element.283, f32[4,4,128,128]{3,2,1,0:T(8,128)} %get-tuple-element.296, s32[]{:T(128)S(6)} %select_n.100, pred[]{:T(512)} %bitcast.73), kind=kLoop, calls=%fused_computation.1.clone.1 | loop fusion | flops 131072 | bytes 786437 | tf_op jit(solution)/shard_map/while/body/jit(_where)/select_n | solution.py:43
  92.2 0.6 dynamic_slice.35
  93.4 1.1 %add_select_fusion.5 = f32[4,128,128]{2,1,0:T(8,128)S(1)} fusion(f32[4,128,128]{2,1,0:T(8,128)S(1)} %get-tuple-element.283, f32[4,4,128,128]{3,2,1,0:T(8,128)} %get-tuple-element.296, s32[]{:T(128)S(6)} %select_n.100, pred[]{:T(512)} %bitcast.73), kind=kLoop, calls=%fused_computation.1.clone.1 | loop fusion | flops 131072 | bytes 786437 | tf_op jit(solution)/shard_map/while/body/jit(_where)/select_n | solution.py:43
  94.8 0.8 copy.73
  95.8 0.8 copy.72
  (34 shorter events, 2.9 us)
Async XLA Ops:
  7.2 0.7 copy-start.5
  7.2 35.2 %all-gather.5.cloned.1.call-start = ((), (), s32[]{:S(2)}) async-start(), calls=%async_computation | async-start | bytes 1310720 | tf_op jit(solution)/shard_map/all_gather | solution.py:18
  8.5 1.1 %copy-start.2 = (bf16[1,256,512]{2,1,0:T(8,128)(2,1)S(1)}, bf16[1,256,512]{2,1,0:T(8,128)(2,1)}, u32[]{:S(2)}) copy-start(bf16[1,256,512]{2,1,0:T(8,128)(2,1)} %param.12) | copy-start | bytes 786436
  11.5 12.6 %copy-start.3 = (bf16[1,256,512]{2,1,0:T(8,128)(2,1)S(1)}, bf16[1,256,512]{2,1,0:T(8,128)(2,1)}, u32[]{:S(2)}) copy-start(bf16[1,256,512]{2,1,0:T(8,128)(2,1)} %param.10) | copy-start | bytes 786436
  11.5 76.0 %all-gather.7.cloned.1.call-start = ((), (), s32[]{:S(2)}) async-start(), calls=%async_computation.1 | async-start | bytes 1310720 | tf_op jit(solution)/shard_map/all_gather | solution.py:18
  12.3 0.7 copy-start.6
  24.1 1.0 copy-start
  42.4 0.7 copy-start.4
  56.4 1.0 copy-start.1
Sparse Core Ops, SparseCore 0:
  11.7 30.6 all-gather.4
  54.6 32.9 all-gather.6
where the time goes:
time: 104 us
  blocking collectives  41.3 us (40%)
  waiting for transfers between devices  22.5 us (22%)
  between operations  14.9 us (14%)
  local copies, waits for them, and re-layouts  10.6 us (10%)
  other arithmetic  7.46 us (7%)
  matrix products  4.65 us (4%)
  loops' own time  2.04 us (2%)
    all_gather x2, waiting for transfers between devices, carried_in(): gathered = jax.tree.map(lambda a: lax.all_gather(a, axis), part)  22.4 us
    psum x1, blocking collectives, shards(): grad_gain = lax.psum(gain_local, ('dp', 'seq'))  21.6 us
    psum x1, blocking collectives, shards(): lax.psum((square_local, jnp.sum(scaled * attended, axis=1)), 'tensor')  9.89 us
    unnamed x1, blocking collectives  9.88 us
    unnamed x23, local copies, waits for them, and re-layouts  7.42 us
    select_n x3, other arithmetic, joined(): jnp.where(later[1] > 0, later[0], earlier[0] + later[0])  3.15 us
  transfers between devices with their start and end apart: 2, of which 2 were waited for; matrix products, arithmetic and copies ran while one was open for 7% of the time, Pallas kernels for 0%

commit v1 on v0

v1 whole, which is shorter than its diff:
```python
import functools

import jax
import jax.numpy as jnp
from jax import lax
from jax.experimental import pallas as pl
from jax.experimental.pallas import tpu as pltpu
from jax.sharding import PartitionSpec as P

DH = 128
BLK = 64
CH = 2048
EPS = 1e-05
CUTS = 2

MESH = pl.DeviceIdType.MESH
F32 = jnp.float32
BF16 = jnp.bfloat16


def dot(a, b, over_a, over_b):
    return lax.dot_general(a, b, (((over_a,), (over_b,)), ((), ())), preferred_element_type=F32)


def kernel(
    sizes, off_ref, gain_ref, q_hbm, k_hbm, v_hbm, g_hbm,
    out_hbm, gq_hbm, gk_hbm, gv_hbm, gg_ref,
    q_ref, k_ref, v_ref, g_ref, out_ref, gq_ref, gk_ref, gv_ref,
    allow_ref, wts_ref, att_ref, pre_ref, pk_ref, pv_ref,
    fsend, frecv, bsend, brecv, stats, gains,
    in_sem, out_sem, fs_sem, fr_sem, bs_sem, br_sem, ss_sem, sr_sem, gs_sem, gr_sem,
):
    n_dp, n_seq, n_ten = sizes
    group = n_dp * n_seq
    length, width = q_ref.shape
    heads = width // DH
    rows = DH // CUTS
    place = lax.axis_index("seq")
    ten = lax.axis_index("tensor")
    mine = lax.axis_index("dp") * n_seq + place
    first, last = place == 0, place == n_seq - 1

    loads = [
        pltpu.make_async_copy(src, dst, in_sem.at[i])
        for i, (src, dst) in enumerate(((k_hbm, k_ref), (v_hbm, v_ref), (q_hbm, q_ref), (g_hbm, g_ref)))
    ]
    for load in loads:
        load.start()

    barrier = pltpu.get_barrier_semaphore()

    def peer(turn):
        other = lax.rem(mine + turn, group)
        return other, {"dp": lax.div(other, n_seq), "seq": lax.rem(other, n_seq)}

    def greet(turn, carry):
        pl.semaphore_signal(barrier, inc=1, device_id=peer(turn)[1], device_id_type=MESH)
        return carry

    lax.fori_loop(1, group, greet, 0)
    for turn in range(1, n_ten):
        pl.semaphore_signal(
            barrier, inc=1, device_id={"tensor": lax.rem(ten + turn, n_ten)}, device_id_type=MESH
        )

    def cols(h):
        return pl.ds(h * DH, DH)

    def forward(c):
        h, at = c // CUTS, pl.ds((c % CUTS) * rows, rows)
        return pltpu.make_async_remote_copy(
            src_ref=fsend.at[h, at], dst_ref=frecv.at[h, at],
            send_sem=fs_sem.at[c], recv_sem=fr_sem.at[c],
            device_id={"seq": place + 1}, device_id_type=MESH,
        )

    def backward(c):
        h, at = c // CUTS, pl.ds((c % CUTS) * rows, rows)
        return pltpu.make_async_remote_copy(
            src_ref=bsend.at[h, at], dst_ref=brecv.at[h, at],
            send_sem=bs_sem.at[c], recv_sem=br_sem.at[c],
            device_id={"seq": place - 1}, device_id_type=MESH,
        )

    starts_at = []
    starts = jnp.int32(0)
    for j in range(off_ref.shape[1]):
        offset = off_ref[0, j]
        starts_at.append(jnp.where(offset < BLK, j * BLK + offset, length))
        starts = starts + jnp.where(offset < BLK, 1, 0)

    def labels(positions):
        total = jnp.zeros(positions.shape, jnp.int32)
        for at in starts_at:
            total = total + jnp.where(positions >= at, 1, 0)
        return total

    label = labels(lax.broadcasted_iota(jnp.int32, (length, DH), 0))
    head_mask = jnp.where(label == 0, 1.0, 0.0).astype(BF16)
    tail_mask = jnp.where(label == starts, 1.0, 0.0).astype(BF16)
    keep = jnp.full((rows, DH), starts, jnp.int32) == 0

    loads[0].wait()
    loads[1].wait()
    for h in range(heads):
        fsend[h] = dot(k_ref[:, cols(h)] * tail_mask, v_ref[:, cols(h)], 0, 0)
        if h == 0:
            pl.semaphore_wait(barrier, group - 1 + n_ten - 1)

        @pl.when(first & (n_seq > 1))
        def _():
            for part in range(CUTS):
                forward(h * CUTS + part).start()

    rows_at = lax.broadcasted_iota(jnp.int32, (length, length), 0)
    cols_at = lax.broadcasted_iota(jnp.int32, (length, length), 1)
    allow_ref[...] = jnp.where(
        (labels(rows_at) == labels(cols_at)) & (cols_at <= rows_at), 1.0, 0.0
    )

    @pl.when(first)
    def _():
        frecv[...] = jnp.zeros_like(frecv)

    @pl.when(last)
    def _():
        brecv[...] = jnp.zeros_like(brecv)

    loads[2].wait()
    loads[3].wait()

    square = jnp.zeros((length, DH), F32)
    raw = jnp.zeros((length, DH), F32)
    for h in range(heads):
        query = q_ref[:, cols(h)]
        scores = dot(query, k_ref[:, cols(h)], 1, 1)
        weights = (scores * allow_ref[...]).astype(BF16)
        wts_ref[h] = weights
        local_out = dot(weights, v_ref[:, cols(h)], 1, 0)

        for part in range(CUTS):
            c = h * CUTS + part

            @pl.when(jnp.logical_not(first))
            def _():
                forward(c).wait_recv()

                @pl.when(jnp.logical_not(last))
                def _():
                    at = pl.ds(part * rows, rows)
                    fsend[h, at] = fsend[h, at] + jnp.where(keep, frecv[h, at], 0.0)
                    forward(c).start()

        carried = frecv[h].astype(BF16)
        attended = local_out + dot(query * head_mask, carried, 1, 0)
        att_ref[:, cols(h)] = attended
        square = square + attended * attended
        raw = raw + gain_ref[:, cols(h)] * g_ref[:, cols(h)].astype(F32) * attended

    stats[ten, 0:1, :] = jnp.sum(square.T, axis=0, keepdims=True)
    stats[ten, 1:2, :] = jnp.sum(raw.T, axis=0, keepdims=True)

    def exchange(turn, slot):
        return pltpu.make_async_remote_copy(
            src_ref=stats.at[slot], dst_ref=stats.at[slot],
            send_sem=ss_sem.at[turn], recv_sem=sr_sem.at[slot],
            device_id={"tensor": lax.rem(ten + turn, n_ten)}, device_id_type=MESH,
        )

    for turn in range(1, n_ten):
        exchange(turn, ten).start()
    for turn in range(1, n_ten):
        exchange(turn, lax.rem(ten + turn, n_ten)).wait_recv()
    totals = stats[0]
    for t in range(1, n_ten):
        totals = totals + stats[t]
    inverse = lax.rsqrt(totals[0:1, :] / CH + EPS)
    slope = inverse * inverse * (totals[1:2, :] / CH)
    inverse = jnp.broadcast_to(inverse, (DH, length)).T
    slope = jnp.broadcast_to(slope, (DH, length)).T

    for h in range(heads):
        upstream = g_ref[:, cols(h)].astype(F32)
        pre = inverse * (gain_ref[:, cols(h)] * upstream - att_ref[:, cols(h)] * slope)
        pre = pre.astype(BF16)
        pre_ref[:, cols(h)] = pre
        bsend[h] = dot(q_ref[:, cols(h)] * head_mask, pre, 0, 0)

        @pl.when(last & (n_seq > 1))
        def _():
            for part in range(CUTS):
                backward(h * CUTS + part).start()

    def store(index, h, src, dst):
        return pltpu.make_async_copy(src.at[:, cols(h)], dst.at[:, cols(h)], out_sem.at[index, h])

    for h in range(heads):
        normed = att_ref[:, cols(h)] * inverse
        out_ref[:, cols(h)] = (gain_ref[:, cols(h)] * normed).astype(BF16)
        store(0, h, out_ref, out_hbm).start()
        gains[mine, :, cols(h)] = jnp.sum(
            g_ref[:, cols(h)].astype(F32) * normed, axis=0, keepdims=True
        )

    def send_gain(turn, slot):
        return pltpu.make_async_remote_copy(
            src_ref=gains.at[slot], dst_ref=gains.at[slot],
            send_sem=gs_sem.at[turn], recv_sem=gr_sem.at[slot],
            device_id=peer(turn)[1], device_id_type=MESH,
        )

    def start_gain(turn, carry):
        send_gain(turn, mine).start()
        return carry

    lax.fori_loop(1, group, start_gain, 0)

    for h in range(heads):
        query, key, value = q_ref[:, cols(h)], k_ref[:, cols(h)], v_ref[:, cols(h)]
        pre = pre_ref[:, cols(h)]
        grad_weights = (dot(pre, value, 1, 1) * allow_ref[...]).astype(BF16)
        gq = dot(grad_weights, key, 1, 0) + dot(pre * head_mask, frecv[h].astype(BF16), 1, 1)
        gq_ref[:, cols(h)] = gq.astype(BF16)
        store(1, h, gq_ref, gq_hbm).start()
        pk_ref[...] = dot(grad_weights, query, 0, 0)
        pv_ref[...] = dot(wts_ref[h], pre, 0, 0)

        for part in range(CUTS):
            c = h * CUTS + part

            @pl.when(jnp.logical_not(last))
            def _():
                backward(c).wait_recv()

                @pl.when(jnp.logical_not(first))
                def _():
                    at = pl.ds(part * rows, rows)
                    bsend[h, at] = bsend[h, at] + jnp.where(keep, brecv[h, at], 0.0)
                    backward(c).start()

        later = brecv[h].astype(BF16)
        gk_ref[:, cols(h)] = (pk_ref[...] + dot(value * tail_mask, later, 1, 1)).astype(BF16)
        store(2, h, gk_ref, gk_hbm).start()
        gv_ref[:, cols(h)] = (pv_ref[...] + dot(key * tail_mask, later, 1, 0)).astype(BF16)
        store(3, h, gv_ref, gv_hbm).start()

    def wait_gain(turn, carry):
        send_gain(turn, peer(turn)[0]).wait_recv()
        return carry

    lax.fori_loop(1, group, wait_gain, 0)
    gg_ref[...] = lax.fori_loop(
        0, group, lambda i, total: total + gains[i], jnp.zeros(gg_ref.shape, F32)
    )

    def sent_gain(turn, carry):
        send_gain(turn, mine).wait_send()
        return carry

    lax.fori_loop(1, group, sent_gain, 0)
    for turn in range(1, n_ten):
        exchange(turn, ten).wait_send()

    @pl.when(jnp.logical_not(last))
    def _():
        for c in range(heads * CUTS):
            forward(c).wait_send()

    @pl.when(jnp.logical_not(first))
    def _():
        for c in range(heads * CUTS):
            backward(c).wait_send()

    for index, (src, dst) in enumerate(
        ((out_ref, out_hbm), (gq_ref, gq_hbm), (gk_ref, gk_hbm), (gv_ref, gv_hbm))
    ):
        for h in range(heads):
            store(index, h, src, dst).wait()


def solution(mesh):
    sizes = (mesh.shape["dp"], mesh.shape["seq"], mesh.shape["tensor"])

    def shards(query, key_rows, value, gain, grad_out, start_offset):
        _, length, width = query.shape
        heads = width // DH
        group = sizes[0] * sizes[1]
        cuts = heads * CUTS
        whole = pl.BlockSpec(memory_space=pl.ANY)
        vmem = pl.BlockSpec(memory_space=pltpu.VMEM)
        rows = jax.ShapeDtypeStruct((length, width), BF16)
        dma = pltpu.SemaphoreType.DMA
        flat = lambda a: a.reshape(length, width)
        *outs, grad_gain = pl.pallas_call(
            functools.partial(kernel, sizes),
            out_shape=(rows,) * 4 + (jax.ShapeDtypeStruct((1, width), F32),),
            in_specs=[pl.BlockSpec(memory_space=pltpu.SMEM), vmem] + [whole] * 4,
            out_specs=(whole,) * 4 + (vmem,),
            scratch_shapes=[pltpu.VMEM((length, width), BF16)] * 8
            + [
                pltpu.VMEM((length, length), F32),
                pltpu.VMEM((heads, length, length), BF16),
                pltpu.VMEM((length, width), F32),
                pltpu.VMEM((length, width), BF16),
                pltpu.VMEM((length, DH), F32),
                pltpu.VMEM((length, DH), F32),
            ]
            + [pltpu.VMEM((heads, DH, DH), F32)] * 4
            + [pltpu.VMEM((sizes[2], 2, length), F32), pltpu.VMEM((group, 1, width), F32)]
            + [dma((4,)), dma((4, heads)), dma((cuts,)), dma((cuts,)), dma((cuts,)), dma((cuts,))]
            + [dma((sizes[2],)), dma((sizes[2],)), dma((group,)), dma((group,))],
            compiler_params=pltpu.CompilerParams(
                collective_id=0, has_side_effects=True, vmem_limit_bytes=40 * 1024 * 1024
            ),
        )(start_offset, gain.reshape(1, width), flat(query), flat(key_rows), flat(value), flat(grad_out))
        return tuple(a.reshape(1, length, width) for a in outs) + (grad_gain.reshape(width),)

    split = P("dp", "seq", "tensor")
    return jax.shard_map(
        shards,
        mesh=mesh,
        in_specs=(split, split, split, P("tensor"), split, P("dp", "seq")),
        out_specs=(split, split, split, split, P("tensor")),
        check_vma=False,
    )
```

time: 104 us -> 47 us (0.45)
  blocking collectives: 41.3 us -> 0 us
  Pallas kernels: 0 us -> 38.2 us
  waiting for transfers between devices: 22.5 us -> 0 us
  between operations: 14.9 us -> 0.66 us
  other arithmetic: 7.46 us -> 0 us
  matrix products: 4.65 us -> 0 us
  local copies, waits for them, and re-layouts: 10.6 us -> 7.86 us
  loops' own time: 2.04 us -> 0 us
    pallas_call x0 -> x1, Pallas kernels: none -> 38.2 us  [shards(): pl.pallas_call(functools.partial(kernel, sizes), out_shape=(rows,) * 4 +...]
    psum x2 -> x0, blocking collectives: 31.5 us -> none  [the longest x1 21.6 us: shards(): grad_gain = lax.psum(gain_local, ('dp', 'seq'))]
    all_gather x2 -> x0, waiting for transfers between devices: 22.4 us -> none  [carried_in(): gathered = jax.tree.map(lambda a: lax.all_gather(a, axis), part)]
    unnamed x1 -> x0, blocking collectives: 9.88 us -> none
    dot_general x12 -> x0, matrix products: 4.65 us -> none  [the longest x1 0.94 us: shards(): jnp.einsum('shi,shj->hij', tail_keys, value_heads, preferred_element_type...]
    select_n x3 -> x0, other arithmetic: 3.15 us -> none  [joined(): jnp.where(later[1] > 0, later[0], earlier[0] + later[0])]
    another operation x2 -> x0, loops' own time: 2.04 us -> none  [carried_in(): return lax.fori_loop(0, ahead, one, state)]
    reduce_sum x3 -> x0, other arithmetic: 1.91 us -> none  [the longest x1 1.19 us: shards(): gain_local = jnp.sum(upstream * normed, axis=0)]
  transfers between devices with their start and end apart: 2 -> 0, of which waited for: 2 -> 0; matrix products, arithmetic and copies ran while one was open for 7% -> 0% of each run, Pallas kernels for 0% -> 0%
where the time goes in v1:
time: 47 us; the launch traced here: 46.7 us
  Pallas kernels  38.2 us (81%)
  local copies, waits for them, and re-layouts  7.86 us (17%)
  between operations  0.66 us (1%)
    pallas_call x1, Pallas kernels, shards(): pl.pallas_call(functools.partial(kernel, sizes), out_shape=(rows,) * 4 +...  38.2 us
    unnamed x17, local copies, waits for them, and re-layouts  7.86 us

profile of v1, /device:TPU:0, one launch (start us, length us, event | category | flops | bytes accessed | tf_op | source)
XLA Modules:
  0.0 46.7 jit_solution(2287294871066451774)
XLA Ops:
  0.6 0.0 copy-start.4
  0.6 0.0 copy-start.5
  0.7 0.7 %copy-done.4 = f32[512]{0:T(512)S(1)} copy-done((f32[512]{0:T(512)S(1)}, f32[512]{0:T(512)}, u32[]{:S(2)}) %copy-start.4) | copy-done | bytes 2072
  1.3 0.0 copy-done.5
  1.3 0.0 copy-start
  1.3 0.9 %copy-done = bf16[1,256,512]{2,1,0:T(8,128)(2,1)S(1)} copy-done((bf16[1,256,512]{2,1,0:T(8,128)(2,1)S(1)}, bf16[1,256,512]{2,1,0:T(8,128)(2,1)}, u32[]{:S(2)}) %copy-start) | copy-done | bytes 262168
  2.3 0.0 copy-start.1
  2.3 0.9 %copy-done.1 = bf16[1,256,512]{2,1,0:T(8,128)(2,1)S(1)} copy-done((bf16[1,256,512]{2,1,0:T(8,128)(2,1)S(1)}, bf16[1,256,512]{2,1,0:T(8,128)(2,1)}, u32[]{:S(2)}) %copy-start.1) | copy-done | bytes 262168
  3.2 0.0 copy-start.2
  3.2 0.9 %copy-done.2 = bf16[1,256,512]{2,1,0:T(8,128)(2,1)S(1)} copy-done((bf16[1,256,512]{2,1,0:T(8,128)(2,1)S(1)}, bf16[1,256,512]{2,1,0:T(8,128)(2,1)}, u32[]{:S(2)}) %copy-start.2) | copy-done | bytes 262168
  4.2 0.0 copy-start.3
  4.2 0.9 %copy-done.3 = bf16[1,256,512]{2,1,0:T(8,128)(2,1)S(1)} copy-done((bf16[1,256,512]{2,1,0:T(8,128)(2,1)S(1)}, bf16[1,256,512]{2,1,0:T(8,128)(2,1)}, u32[]{:S(2)}) %copy-start.3) | copy-done | bytes 262168
  5.1 38.2 %shard_map.101 = (bf16[256,512]{1,0:T(8,128)(2,1)S(1)}, bf16[256,512]{1,0:T(8,128)(2,1)S(1)}, bf16[256,512]{1,0:T(8,128)(2,1)S(1)}, bf16[256,512]{1,0:T(8,128)(2,1)S(1)}, f32[1,512]{1,0:T(1,128)S(1)}) custom-call(s32[1,4]{1,0:T(1,128)S(1)} %copy-done.5, f32[1,512]{1,0:T(1,128)S(1)} %bitcast.18, bf16[256,512]{1,0:T(8,128)(2,1)S(1)} %bitcast.14, ...), custom_call_target="tpu_custom_call" | custom-call | tf_op jit(solution)/shard_map/pallas_call | solution.py:294
  43.3 0.7 %copy.16 = bf16[1,256,512]{2,1,0:T(8,128)(2,1)} copy(bf16[1,256,512]{2,1,0:T(8,128)(2,1)S(1)} %bitcast.13) | data formatting | bytes 524288
  44.0 0.7 %copy.17 = bf16[1,256,512]{2,1,0:T(8,128)(2,1)} copy(bf16[1,256,512]{2,1,0:T(8,128)(2,1)S(1)} %bitcast.12) | data formatting | bytes 524288
  44.7 0.7 %copy.18 = bf16[1,256,512]{2,1,0:T(8,128)(2,1)} copy(bf16[1,256,512]{2,1,0:T(8,128)(2,1)S(1)} %bitcast.11) | data formatting | bytes 524288
  45.4 0.7 %copy.19 = bf16[1,256,512]{2,1,0:T(8,128)(2,1)} copy(bf16[1,256,512]{2,1,0:T(8,128)(2,1)S(1)} %bitcast.10) | data formatting | bytes 524288
  46.1 0.6 %copy.20 = f32[512]{0:T(512)} copy(f32[512]{0:T(512)S(1)} %bitcast.19) | data formatting | bytes 4096
Async XLA Ops:
  0.6 0.7 %copy-start.4 = (f32[512]{0:T(512)S(1)}, f32[512]{0:T(512)}, u32[]{:S(2)}) copy-start(f32[512]{0:T(512)} %param.9) | copy-start | bytes 6148
  0.6 0.7 %copy-start.5 = (s32[1,4]{1,0:T(1,128)S(1)}, s32[1,4]{1,0:T(1,128)}, u32[]{:S(2)}) copy-start(s32[1,4]{1,0:T(1,128)} %off_ref.1) | copy-start | bytes 52
  1.3 1.0 %copy-start = (bf16[1,256,512]{2,1,0:T(8,128)(2,1)S(1)}, bf16[1,256,512]{2,1,0:T(8,128)(2,1)}, u32[]{:S(2)}) copy-start(bf16[1,256,512]{2,1,0:T(8,128)(2,1)} %param.6) | copy-start | bytes 786436
  2.3 0.9 %copy-start.1 = (bf16[1,256,512]{2,1,0:T(8,128)(2,1)S(1)}, bf16[1,256,512]{2,1,0:T(8,128)(2,1)}, u32[]{:S(2)}) copy-start(bf16[1,256,512]{2,1,0:T(8,128)(2,1)} %param.7) | copy-start | bytes 786436
  3.2 0.9 %copy-start.2 = (bf16[1,256,512]{2,1,0:T(8,128)(2,1)S(1)}, bf16[1,256,512]{2,1,0:T(8,128)(2,1)}, u32[]{:S(2)}) copy-start(bf16[1,256,512]{2,1,0:T(8,128)(2,1)} %param.8) | copy-start | bytes 786436
  4.2 0.9 %copy-start.3 = (bf16[1,256,512]{2,1,0:T(8,128)(2,1)S(1)}, bf16[1,256,512]{2,1,0:T(8,128)(2,1)}, u32[]{:S(2)}) copy-start(bf16[1,256,512]{2,1,0:T(8,128)(2,1)} %param.10) | copy-start | bytes 786436

commit v2 on v1

v2 whole, which is shorter than its diff:
```python
import functools

import jax
import jax.numpy as jnp
from jax import lax
from jax.experimental import pallas as pl
from jax.experimental.pallas import tpu as pltpu
from jax.sharding import PartitionSpec as P

DH = 128
BLK = 64
CH = 2048
EPS = 1e-05
CUTS = 2

MESH = pl.DeviceIdType.MESH
F32 = jnp.float32
BF16 = jnp.bfloat16


def dot(a, b, over_a, over_b):
    return lax.dot_general(a, b, (((over_a,), (over_b,)), ((), ())), preferred_element_type=F32)


def kernel(
    sizes, off_hbm, gain_hbm, q_hbm, k_hbm, v_hbm, g_hbm,
    out_ref, gq_ref, gk_ref, gv_ref, gg_ref,
    off_ref, gain_ref, q_ref, k_ref, v_ref, g_ref,
    allow_ref, head_ref, tail_ref, wts_ref, att_ref, pre_ref, pk_ref, pv_ref, sq_ref, raw_ref,
    fsend, frecv, bsend, brecv, stats, gains,
    in_sem, fs_sem, fr_sem, bs_sem, br_sem, ss_sem, sr_sem, gs_sem, gr_sem,
):
    n_dp, n_seq, n_ten = sizes
    group = n_dp * n_seq
    length, width = q_ref.shape
    heads = width // DH
    rows = DH // CUTS
    place = lax.axis_index("seq")
    ten = lax.axis_index("tensor")
    mine = lax.axis_index("dp") * n_seq + place
    first, last = place == 0, place == n_seq - 1

    loads = [
        pltpu.make_async_copy(src, dst, in_sem.at[i])
        for i, (src, dst) in enumerate(
            (
                (off_hbm, off_ref), (k_hbm, k_ref), (v_hbm, v_ref),
                (q_hbm, q_ref), (g_hbm, g_ref), (gain_hbm, gain_ref),
            )
        )
    ]
    for load in loads:
        load.start()

    barrier = pltpu.get_barrier_semaphore()

    def peer(turn):
        other = lax.rem(mine + turn, group)
        return other, {"dp": lax.div(other, n_seq), "seq": lax.rem(other, n_seq)}

    def greet(turn, carry):
        pl.semaphore_signal(barrier, inc=1, device_id=peer(turn)[1], device_id_type=MESH)
        return carry

    lax.fori_loop(1, group, greet, 0)
    for turn in range(1, n_ten):
        pl.semaphore_signal(
            barrier, inc=1, device_id={"tensor": lax.rem(ten + turn, n_ten)}, device_id_type=MESH
        )

    def cols(h):
        return pl.ds(h * DH if isinstance(h, int) else pl.multiple_of(h * DH, DH), DH)

    def piece(part):
        return pl.ds(part * rows, rows)

    def forward(h, part):
        return pltpu.make_async_remote_copy(
            src_ref=fsend.at[h, piece(part)], dst_ref=frecv.at[h, piece(part)],
            send_sem=fs_sem.at[h, part], recv_sem=fr_sem.at[h, part],
            device_id={"seq": place + 1}, device_id_type=MESH,
        )

    def backward(h, part):
        return pltpu.make_async_remote_copy(
            src_ref=bsend.at[h, piece(part)], dst_ref=brecv.at[h, piece(part)],
            send_sem=bs_sem.at[h, part], recv_sem=br_sem.at[h, part],
            device_id={"seq": place - 1}, device_id_type=MESH,
        )

    def each_head(body):
        def step(h, carry):
            body(h)
            return carry

        lax.fori_loop(0, heads, step, 0)

    loads[0].wait()
    starts_at = []
    starts = jnp.int32(0)
    for j in range(off_ref.shape[1]):
        offset = off_ref[0, j]
        starts_at.append(jnp.where(offset < BLK, j * BLK + offset, length))
        starts = starts + jnp.where(offset < BLK, 1, 0)

    def labels(positions):
        total = jnp.zeros(positions.shape, jnp.int32)
        for at in starts_at:
            total = total + jnp.where(positions >= at, 1, 0)
        return total

    label = labels(lax.broadcasted_iota(jnp.int32, (length, DH), 0))
    head_ref[...] = jnp.where(label == 0, 1.0, 0.0).astype(BF16)
    tail_ref[...] = jnp.where(label == starts, 1.0, 0.0).astype(BF16)

    def passed(own, come):
        keep = jnp.full(come.shape, starts, jnp.int32) == 0
        return own + jnp.where(keep, come, 0.0)

    loads[1].wait()
    loads[2].wait()

    def tail(h):
        fsend[h] = dot(k_ref[:, cols(h)] * tail_ref[...], v_ref[:, cols(h)], 0, 0)

    def launch(h):
        @pl.when(first & (n_seq > 1))
        def _():
            for part in range(CUTS):
                forward(h, part).start()

    tail(0)
    pl.semaphore_wait(barrier, group - 1 + n_ten - 1)
    launch(0)

    def tails(h, carry):
        tail(h)
        launch(h)
        return carry

    lax.fori_loop(1, heads, tails, 0)

    rows_at = lax.broadcasted_iota(jnp.int32, (length, length), 0)
    cols_at = lax.broadcasted_iota(jnp.int32, (length, length), 1)
    allow_ref[...] = jnp.where(
        (labels(rows_at) == labels(cols_at)) & (cols_at <= rows_at), 1.0, 0.0
    )

    @pl.when(first)
    def _():
        frecv[...] = jnp.zeros_like(frecv)

    @pl.when(last)
    def _():
        brecv[...] = jnp.zeros_like(brecv)

    sq_ref[...] = jnp.zeros_like(sq_ref)
    raw_ref[...] = jnp.zeros_like(raw_ref)
    for load in loads[3:]:
        load.wait()

    def relay_right(h, part):
        @pl.when(jnp.logical_not(first))
        def _():
            forward(h, part).wait_recv()

            @pl.when(jnp.logical_not(last))
            def _():
                fsend[h, piece(part)] = passed(fsend[h, piece(part)], frecv[h, piece(part)])
                forward(h, part).start()

    def attend(h):
        relay_right(h, 0)
        scores = dot(q_ref[:, cols(h)], k_ref[:, cols(h)], 1, 1)
        wts_ref[h] = (scores * allow_ref[...]).astype(BF16)
        att_ref[:, cols(h)] = dot(wts_ref[h], v_ref[:, cols(h)], 1, 0)
        for part in range(1, CUTS):
            relay_right(h, part)
        attended = att_ref[:, cols(h)] + dot(
            q_ref[:, cols(h)] * head_ref[...], frecv[h].astype(BF16), 1, 0
        )
        att_ref[:, cols(h)] = attended
        sq_ref[...] = sq_ref[...] + attended * attended
        raw_ref[...] = raw_ref[...] + gain_ref[:, cols(h)] * g_ref[:, cols(h)].astype(F32) * attended

    each_head(attend)

    stats[ten, 0:1, :] = jnp.sum(sq_ref[...].T, axis=0, keepdims=True)
    stats[ten, 1:2, :] = jnp.sum(raw_ref[...].T, axis=0, keepdims=True)

    def exchange(turn, slot):
        return pltpu.make_async_remote_copy(
            src_ref=stats.at[slot], dst_ref=stats.at[slot],
            send_sem=ss_sem.at[turn], recv_sem=sr_sem.at[slot],
            device_id={"tensor": lax.rem(ten + turn, n_ten)}, device_id_type=MESH,
        )

    for turn in range(1, n_ten):
        exchange(turn, ten).start()
    for turn in range(1, n_ten):
        exchange(turn, lax.rem(ten + turn, n_ten)).wait_recv()
    totals = stats[0]
    for t in range(1, n_ten):
        totals = totals + stats[t]
    inverse = lax.rsqrt(totals[0:1, :] / CH + EPS)
    slope = inverse * inverse * (totals[1:2, :] / CH)
    sq_ref[...] = jnp.broadcast_to(inverse, (DH, length)).T
    raw_ref[...] = jnp.broadcast_to(slope, (DH, length)).T

    def before_norm(h):
        upstream = g_ref[:, cols(h)].astype(F32)
        pre = sq_ref[...] * (gain_ref[:, cols(h)] * upstream - att_ref[:, cols(h)] * raw_ref[...])
        pre = pre.astype(BF16)
        pre_ref[:, cols(h)] = pre
        bsend[h] = dot(q_ref[:, cols(h)] * head_ref[...], pre, 0, 0)

        @pl.when(last & (n_seq > 1))
        def _():
            for part in range(CUTS):
                backward(h, part).start()

    each_head(before_norm)

    def after_norm(h):
        normed = att_ref[:, cols(h)] * sq_ref[...]
        out_ref[:, cols(h)] = (gain_ref[:, cols(h)] * normed).astype(BF16)
        gains[mine, :, cols(h)] = jnp.sum(
            g_ref[:, cols(h)].astype(F32) * normed, axis=0, keepdims=True
        )

    for h in range(heads):
        after_norm(h)

    def send_gain(turn, slot):
        return pltpu.make_async_remote_copy(
            src_ref=gains.at[slot], dst_ref=gains.at[slot],
            send_sem=gs_sem.at[turn], recv_sem=gr_sem.at[slot],
            device_id=peer(turn)[1], device_id_type=MESH,
        )

    def start_gain(turn, carry):
        send_gain(turn, mine).start()
        return carry

    lax.fori_loop(1, group, start_gain, 0)

    def relay_left(h, part):
        @pl.when(jnp.logical_not(last))
        def _():
            backward(h, part).wait_recv()

            @pl.when(jnp.logical_not(first))
            def _():
                bsend[h, piece(part)] = passed(bsend[h, piece(part)], brecv[h, piece(part)])
                backward(h, part).start()

    def local_query(h):
        pre = pre_ref[:, cols(h)]
        grad_weights = (dot(pre, v_ref[:, cols(h)], 1, 1) * allow_ref[...]).astype(BF16)
        gq = dot(grad_weights, k_ref[:, cols(h)], 1, 0)
        gq = gq + dot(pre * head_ref[...], frecv[h].astype(BF16), 1, 1)
        gq_ref[:, cols(h)] = gq.astype(BF16)
        pk_ref[:, cols(h)] = dot(grad_weights, q_ref[:, cols(h)], 0, 0)

    def local_value(h):
        pv_ref[:, cols(h)] = dot(wts_ref[h], pre_ref[:, cols(h)], 0, 0)

    def finish(h):
        later = brecv[h].astype(BF16)
        gk = pk_ref[:, cols(h)] + dot(v_ref[:, cols(h)] * tail_ref[...], later, 1, 1)
        gk_ref[:, cols(h)] = gk.astype(BF16)
        gv = pv_ref[:, cols(h)] + dot(k_ref[:, cols(h)] * tail_ref[...], later, 1, 0)
        gv_ref[:, cols(h)] = gv.astype(BF16)

    @pl.when(first | last)
    def _():
        def local(h):
            local_query(h)
            local_value(h)

        each_head(local)

        def arrive(h):
            for part in range(CUTS):
                relay_left(h, part)
            finish(h)

        each_head(arrive)

    @pl.when(jnp.logical_not(first | last))
    def _():
        def both(h):
            relay_left(h, 0)
            local_query(h)
            for part in range(1, CUTS):
                relay_left(h, part)
            local_value(h)
            finish(h)

        each_head(both)

    def wait_gain(turn, carry):
        send_gain(turn, peer(turn)[0]).wait_recv()
        return carry

    lax.fori_loop(1, group, wait_gain, 0)
    gg_ref[...] = lax.fori_loop(
        0, group, lambda i, total: total + gains[i], jnp.zeros(gg_ref.shape, F32)
    )

    def sent_gain(turn, carry):
        send_gain(turn, mine).wait_send()
        return carry

    lax.fori_loop(1, group, sent_gain, 0)
    for turn in range(1, n_ten):
        exchange(turn, ten).wait_send()

    @pl.when(jnp.logical_not(last))
    def _():
        for h in range(heads):
            for part in range(CUTS):
                forward(h, part).wait_send()

    @pl.when(jnp.logical_not(first))
    def _():
        for h in range(heads):
            for part in range(CUTS):
                backward(h, part).wait_send()


def hand_out(*refs):
    count = len(refs) // 2
    copies = [
        pltpu.make_async_copy(refs[i], refs[count + i], refs[-1].at[i]) for i in range(count)
    ]
    for copy in copies:
        copy.start()
    for copy in copies:
        copy.wait()


def solution(mesh):
    sizes = (mesh.shape["dp"], mesh.shape["seq"], mesh.shape["tensor"])

    def shards(query, key_rows, value, gain, grad_out, start_offset):
        _, length, width = query.shape
        heads = width // DH
        group = sizes[0] * sizes[1]
        hbm = pl.BlockSpec(memory_space=pltpu.HBM)
        vmem = pl.BlockSpec(memory_space=pltpu.VMEM)
        rows = jax.ShapeDtypeStruct((length, width), BF16)
        shapes = (rows,) * 4 + (jax.ShapeDtypeStruct((1, width), F32),)
        dma = pltpu.SemaphoreType.DMA
        flat = lambda a: a.reshape(length, width)
        outs = pl.pallas_call(
            functools.partial(kernel, sizes),
            out_shape=tuple(pltpu.VMEM(a.shape, a.dtype) for a in shapes),
            in_specs=[hbm] * 6,
            out_specs=(vmem,) * 5,
            scratch_shapes=[pltpu.SMEM(start_offset.shape, jnp.int32), pltpu.VMEM((1, width), F32)]
            + [pltpu.VMEM((length, width), BF16)] * 4
            + [
                pltpu.VMEM((length, length), F32),
                pltpu.VMEM((length, DH), BF16),
                pltpu.VMEM((length, DH), BF16),
                pltpu.VMEM((heads, length, length), BF16),
                pltpu.VMEM((length, width), F32),
                pltpu.VMEM((length, width), BF16),
                pltpu.VMEM((length, width), F32),
                pltpu.VMEM((length, width), F32),
                pltpu.VMEM((length, DH), F32),
                pltpu.VMEM((length, DH), F32),
            ]
            + [pltpu.VMEM((heads, DH, DH), F32)] * 4
            + [pltpu.VMEM((sizes[2], 2, length), F32), pltpu.VMEM((group, 1, width), F32)]
            + [dma((6,))] + [dma((heads, CUTS))] * 4
            + [dma((sizes[2],)), dma((sizes[2],)), dma((group,)), dma((group,))],
            compiler_params=pltpu.CompilerParams(
                collective_id=0, has_side_effects=True, vmem_limit_bytes=61 * 1024 * 1024
            ),
        )(start_offset, gain.reshape(1, width), flat(query), flat(key_rows), flat(value), flat(grad_out))
        *outs, grad_gain = pl.pallas_call(
            hand_out,
            out_shape=shapes,
            in_specs=[pl.BlockSpec(memory_space=pl.ANY)] * 5,
            out_specs=(hbm,) * 5,
            scratch_shapes=[dma((5,))],
        )(*outs)
        return tuple(a.reshape(1, length, width) for a in outs) + (grad_gain.reshape(width),)

    split = P("dp", "seq", "tensor")
    return jax.shard_map(
        shards,
        mesh=mesh,
        in_specs=(split, split, split, P("tensor"), split, P("dp", "seq")),
        out_specs=(split, split, split, split, P("tensor")),
        check_vma=False,
    )
```

time: 47 us -> 73 us (1.55)
  Pallas kernels: 38.2 us -> 68.8 us
  local copies, waits for them, and re-layouts: 7.86 us -> 3.37 us
    pallas_call x1 -> x2, Pallas kernels: 38.2 us -> 68.8 us  [the longest x1 35.9 us: shards(): pl.pallas_call(functools.partial(kernel, sizes), out_shape=tuple((pltpu.V...]
    unnamed x17 -> x10, local copies, waits for them, and re-layouts: 7.86 us -> 3.37 us
where the time goes in v2:
time: 73 us; the launch traced here: 72.8 us
  Pallas kernels  68.8 us (94%)
  local copies, waits for them, and re-layouts  3.37 us (5%)
    pallas_call x1, Pallas kernels, shards(): pl.pallas_call(functools.partial(kernel, sizes), out_shape=tuple((pltpu.V...  35.9 us
    pallas_call x1, Pallas kernels, shards(): pl.pallas_call(hand_out, out_shape=shapes, in_specs=[pl.BlockSpec(memory_...  33 us
    unnamed x10, local copies, waits for them, and re-layouts  3.37 us

profile of v2, /device:TPU:0, one launch (start us, length us, event | category | flops | bytes accessed | tf_op | source)
XLA Modules:
  0.0 72.8 jit_solution(4465758084033881048)
XLA Ops:
  0.6 35.9 %shard_map.101 = (bf16[256,512]{1,0:T(8,128)(2,1)S(1)}, bf16[256,512]{1,0:T(8,128)(2,1)S(1)}, bf16[256,512]{1,0:T(8,128)(2,1)S(1)}, bf16[256,512]{1,0:T(8,128)(2,1)S(1)}, f32[1,512]{1,0:T(1,128)S(1)}) custom-call(s32[1,4]{1,0:T(1,128)} %off_hbm.1, f32[1,512]{1,0:T(1,128)} %bitcast.14, bf16[256,512]{1,0:T(8,128)(2,1)} %bitcast.10, bf16[256,512]{1,0:T(8,128)(2,1)} %bitcast.11, ...), custom_call_target="tpu_custom_call" | custom-call | tf_op jit(solution)/shard_map/pallas_call | solution.py:356
  36.5 0.0 copy-start
  36.5 0.7 copy-done
  37.2 0.0 copy-start.1
  37.2 0.7 copy-done.1
  37.9 0.0 copy-start.2
  37.9 0.7 copy-done.2
  38.6 0.0 copy-start.3
  38.6 0.7 copy-done.3
  39.3 0.0 copy-start.4
  39.3 0.6 copy-done.4
  39.9 33.0 %shard_map.102 = (bf16[256,512]{1,0:T(8,128)(2,1)}, bf16[256,512]{1,0:T(8,128)(2,1)}, bf16[256,512]{1,0:T(8,128)(2,1)}, bf16[256,512]{1,0:T(8,128)(2,1)}, f32[1,512]{1,0:T(1,128)}) custom-call(bf16[256,512]{1,0:T(8,128)(2,1)} %copy-done, bf16[256,512]{1,0:T(8,128)(2,1)} %copy-done.1, bf16[256,512]{1,0:T(8,128)(2,1)} %copy-done.2, ...), custom_call_target="tpu_custom_call" | custom-call | tf_op jit(solution)/shard_map/pallas_call | solution.py:383
Async XLA Ops:
  36.5 0.7 copy-start
  37.2 0.7 copy-start.1
  37.9 0.7 copy-start.2
  38.6 0.7 copy-start.3
  39.3 0.6 copy-start.4

commit v3 on v2

--- a/solution.py
+++ b/solution.py
@@ -27,17 +27,16 @@
     out_ref, gq_ref, gk_ref, gv_ref, gg_ref,
     off_ref, gain_ref, q_ref, k_ref, v_ref, g_ref,
     allow_ref, head_ref, tail_ref, wts_ref, att_ref, pre_ref, pk_ref, pv_ref, sq_ref, raw_ref,
-    fsend, frecv, bsend, brecv, stats, gains,
-    in_sem, fs_sem, fr_sem, bs_sem, br_sem, ss_sem, sr_sem, gs_sem, gr_sem,
+    fsend, frecv, bsend, brecv, stats, gain_own, gain_come, gain_dp, gain_all,
+    in_sem, fs_sem, fr_sem, bs_sem, br_sem, ss_sem, sr_sem, left_sem, dp_sem, right_sem,
 ):
     n_dp, n_seq, n_ten = sizes
-    group = n_dp * n_seq
     length, width = q_ref.shape
     heads = width // DH
     rows = DH // CUTS
     place = lax.axis_index("seq")
     ten = lax.axis_index("tensor")
-    mine = lax.axis_index("dp") * n_seq + place
+    mine = lax.axis_index("dp")
     first, last = place == 0, place == n_seq - 1
 
     loads = [
@@ -54,19 +53,22 @@
 
     barrier = pltpu.get_barrier_semaphore()
 
-    def peer(turn):
-        other = lax.rem(mine + turn, group)
-        return other, {"dp": lax.div(other, n_seq), "seq": lax.rem(other, n_seq)}
-
-    def greet(turn, carry):
-        pl.semaphore_signal(barrier, inc=1, device_id=peer(turn)[1], device_id_type=MESH)
-        return carry
-
-    lax.fori_loop(1, group, greet, 0)
+    def greet(device):
+        pl.semaphore_signal(barrier, inc=1, device_id=device, device_id_type=MESH)
+
+    @pl.when(jnp.logical_not(last))
+    def _():
+        greet({"seq": place + 1})
+
+    @pl.when(jnp.logical_not(first))
+    def _():
+        greet({"seq": place - 1})
+
     for turn in range(1, n_ten):
-        pl.semaphore_signal(
-            barrier, inc=1, device_id={"tensor": lax.rem(ten + turn, n_ten)}, device_id_type=MESH
-        )
+        greet({"tensor": lax.rem(ten + turn, n_ten)})
+    for turn in range(1, n_dp):
+        greet({"dp": lax.rem(mine + turn, n_dp)})
+    greeted = n_ten - 1 + n_dp - 1 + jnp.where(last, 0, 1) + jnp.where(first, 0, 1)
 
     def cols(h):
         return pl.ds(h * DH if isinstance(h, int) else pl.multiple_of(h * DH, DH), DH)
@@ -130,7 +132,7 @@
                 forward(h, part).start()
 
     tail(0)
-    pl.semaphore_wait(barrier, group - 1 + n_ten - 1)
+    pl.semaphore_wait(barrier, greeted)
     launch(0)
 
     def tails(h, carry):
@@ -170,12 +172,11 @@
                 forward(h, part).start()
 
     def attend(h):
-        relay_right(h, 0)
         scores = dot(q_ref[:, cols(h)], k_ref[:, cols(h)], 1, 1)
         wts_ref[h] = (scores * allow_ref[...]).astype(BF16)
         att_ref[:, cols(h)] = dot(wts_ref[h], v_ref[:, cols(h)], 1, 0)
-        for part in range(1, CUTS):
-            relay_right(h, part)
+
+    def add_carried(h):
         attended = att_ref[:, cols(h)] + dot(
             q_ref[:, cols(h)] * head_ref[...], frecv[h].astype(BF16), 1, 0
         )
@@ -183,7 +184,28 @@
         sq_ref[...] = sq_ref[...] + attended * attended
         raw_ref[...] = raw_ref[...] + gain_ref[:, cols(h)] * g_ref[:, cols(h)].astype(F32) * attended
 
-    each_head(attend)
+    def staggered(ahead, local, relay, finish):
+        def before(h, carry):
+            local(h)
+            return carry
+
+        lax.fori_loop(0, ahead, before, 0)
+
+        def step(h):
+            relay(h, 0)
+
+            @pl.when(h + ahead < heads)
+            def _():
+                local(h + ahead)
+
+            for part in range(1, CUTS):
+                relay(h, part)
+            finish(h)
+
+        each_head(step)
+
+    ahead = jnp.where(first | last, heads, jnp.minimum(place, heads))
+    staggered(ahead, attend, relay_right, add_carried)
 
     stats[ten, 0:1, :] = jnp.sum(sq_ref[...].T, axis=0, keepdims=True)
     stats[ten, 1:2, :] = jnp.sum(raw_ref[...].T, axis=0, keepdims=True)
@@ -224,25 +246,68 @@
     def after_norm(h):
         normed = att_ref[:, cols(h)] * sq_ref[...]
         out_ref[:, cols(h)] = (gain_ref[:, cols(h)] * normed).astype(BF16)
-        gains[mine, :, cols(h)] = jnp.sum(
+        gain_own[:, cols(h)] = jnp.sum(
             g_ref[:, cols(h)].astype(F32) * normed, axis=0, keepdims=True
         )
 
     for h in range(heads):
         after_norm(h)
 
-    def send_gain(turn, slot):
+    gain_left = pltpu.make_async_remote_copy(
+        src_ref=gain_own, dst_ref=gain_come, send_sem=left_sem.at[0], recv_sem=left_sem.at[1],
+        device_id={"seq": place - 1}, device_id_type=MESH,
+    )
+    gain_right = pltpu.make_async_remote_copy(
+        src_ref=gain_all, dst_ref=gain_all, send_sem=right_sem.at[0], recv_sem=right_sem.at[1],
+        device_id={"seq": place + 1}, device_id_type=MESH,
+    )
+
+    def across(turn, slot):
         return pltpu.make_async_remote_copy(
-            src_ref=gains.at[slot], dst_ref=gains.at[slot],
-            send_sem=gs_sem.at[turn], recv_sem=gr_sem.at[slot],
-            device_id=peer(turn)[1], device_id_type=MESH,
-        )
-
-    def start_gain(turn, carry):
-        send_gain(turn, mine).start()
-        return carry
-
-    lax.fori_loop(1, group, start_gain, 0)
+            src_ref=gain_dp.at[slot], dst_ref=gain_dp.at[slot],
+            send_sem=dp_sem.at[0, turn], recv_sem=dp_sem.at[1, slot],
+            device_id={"dp": lax.rem(mine + turn, n_dp)}, device_id_type=MESH,
+        )
+
+    def gain_relay():
+        @pl.when(jnp.logical_not(last))
+        def _():
+            gain_left.wait_recv()
+            gain_own[...] = gain_own[...] + gain_come[...]
+
+        @pl.when(jnp.logical_not(first))
+        def _():
+            gain_left.start()
+
+        @pl.when(first)
+        def _():
+            gain_dp[mine] = gain_own[...]
+            for turn in range(1, n_dp):
+                across(turn, mine).start()
+
+    def gain_total():
+        @pl.when(first)
+        def _():
+            for turn in range(1, n_dp):
+                across(turn, lax.rem(mine + turn, n_dp)).wait_recv()
+            total = gain_dp[0]
+            for i in range(1, n_dp):
+                total = total + gain_dp[i]
+            gain_all[...] = total
+
+        @pl.when(jnp.logical_not(first))
+        def _():
+            gain_right.wait_recv()
+
+        @pl.when(jnp.logical_not(last))
+        def _():
+            gain_right.start()
+
+        gg_ref[...] = gain_all[...]
+
+    @pl.when(last)
+    def _():
+        gain_relay()
 
     def relay_left(h, part):
         @pl.when(jnp.logical_not(last))
@@ -254,7 +319,7 @@
                 bsend[h, piece(part)] = passed(bsend[h, piece(part)], brecv[h, piece(part)])
                 backward(h, part).start()
 
-    def local_query(h):
+    def local_grads(h):
         pre = pre_ref[:, cols(h)]
         grad_weights = (dot(pre, v_ref[:, cols(h)], 1, 1) * allow_ref[...]).astype(BF16)
         gq = dot(grad_weights, k_ref[:, cols(h)], 1, 0)
@@ -262,8 +327,7 @@
         gq_ref[:, cols(h)] = gq.astype(BF16)
         pk_ref[:, cols(h)] = dot(grad_weights, q_ref[:, cols(h)], 0, 0)
 
-    def local_value(h):
-        pv_ref[:, cols(h)] = dot(wts_ref[h], pre_ref[:, cols(h)], 0, 0)
+        pv_ref[:, cols(h)] = dot(wts_ref[h], pre, 0, 0)
 
     def finish(h):
         later = brecv[h].astype(BF16)
@@ -272,47 +336,19 @@
         gv = pv_ref[:, cols(h)] + dot(k_ref[:, cols(h)] * tail_ref[...], later, 1, 0)
         gv_ref[:, cols(h)] = gv.astype(BF16)
 
-    @pl.when(first | last)
-    def _():
-        def local(h):
-            local_query(h)
-            local_value(h)
-
-        each_head(local)
-
-        def arrive(h):
-            for part in range(CUTS):
-                relay_left(h, part)
-            finish(h)
-
-        each_head(arrive)
-
-    @pl.when(jnp.logical_not(first | last))
-    def _():
-        def both(h):
-            relay_left(h, 0)
-            local_query(h)
-            for part in range(1, CUTS):
-                relay_left(h, part)
-            local_value(h)
-            finish(h)
-
-        each_head(both)
-
-    def wait_gain(turn, carry):
-        send_gain(turn, peer(turn)[0]).wait_recv()
-        return carry
-
-    lax.fori_loop(1, group, wait_gain, 0)
-    gg_ref[...] = lax.fori_loop(
-        0, group, lambda i, total: total + gains[i], jnp.zeros(gg_ref.shape, F32)
-    )
-
-    def sent_gain(turn, carry):
-        send_gain(turn, mine).wait_send()
-        return carry
-
-    lax.fori_loop(1, group, sent_gain, 0)
+        @pl.when((h == jnp.where(first, heads - 2, heads // 2 - 1)) & jnp.logical_not(last))
+        def _():
+            gain_relay()
+
+    ahead = jnp.where(last, heads, jnp.minimum(n_seq - place, heads))
+    staggered(ahead, local_grads, relay_left, finish)
+    gain_total()
+
+    @pl.when(first)
+    def _():
+        for turn in range(1, n_dp):
+            across(turn, mine).wait_send()
+
     for turn in range(1, n_ten):
         exchange(turn, ten).wait_send()
 
@@ -321,12 +357,14 @@
         for h in range(heads):
             for part in range(CUTS):
                 forward(h, part).wait_send()
+        gain_right.wait_send()
 
     @pl.when(jnp.logical_not(first))
     def _():
         for h in range(heads):
             for part in range(CUTS):
                 backward(h, part).wait_send()
+        gain_left.wait_send()
 
 
 def hand_out(*refs):
@@ -346,7 +384,6 @@
     def shards(query, key_rows, value, gain, grad_out, start_offset):
         _, length, width = query.shape
         heads = width // DH
-        group = sizes[0] * sizes[1]
         hbm = pl.BlockSpec(memory_space=pltpu.HBM)
         vmem = pl.BlockSpec(memory_space=pltpu.VMEM)
         rows = jax.ShapeDtypeStruct((length, width), BF16)
@@ -373,9 +410,10 @@
                 pltpu.VMEM((length, DH), F32),
             ]
             + [pltpu.VMEM((heads, DH, DH), F32)] * 4
-            + [pltpu.VMEM((sizes[2], 2, length), F32), pltpu.VMEM((group, 1, width), F32)]
+            + [pltpu.VMEM((sizes[2], 2, length), F32), pltpu.VMEM((1, width), F32), pltpu.VMEM((1, width), F32)]
+            + [pltpu.VMEM((sizes[0], 1, width), F32), pltpu.VMEM((1, width), F32)]
             + [dma((6,))] + [dma((heads, CUTS))] * 4
-            + [dma((sizes[2],)), dma((sizes[2],)), dma((group,)), dma((group,))],
+            + [dma((sizes[2],)), dma((sizes[2],)), dma((2,)), dma((2, sizes[0])), dma((2,))],
             compiler_params=pltpu.CompilerParams(
                 collective_id=0, has_side_effects=True, vmem_limit_bytes=61 * 1024 * 1024
             ),
@@ -383,9 +421,10 @@
         *outs, grad_gain = pl.pallas_call(
             hand_out,
             out_shape=shapes,
-            in_specs=[pl.BlockSpec(memory_space=pl.ANY)] * 5,
+            in_specs=[vmem] * 5,
             out_specs=(hbm,) * 5,
             scratch_shapes=[dma((5,))],
+            compiler_params=pltpu.CompilerParams(vmem_limit_bytes=8 * 1024 * 1024),
         )(*outs)
         return tuple(a.reshape(1, length, width) for a in outs) + (grad_gain.reshape(width),)
 

time: 73 us -> 40 us (0.55)
  the two profiles are of different devices: /device:TPU:0 before, /device:TPU:24 now
where the time goes in v3:
time: 40 us; the launch traced here: 39.8 us
  Pallas kernels  39.2 us (98%)
  between operations  0.64 us (2%)
    pallas_call x1, Pallas kernels, shards(): pl.pallas_call(functools.partial(kernel, sizes), out_shape=tuple((pltpu.V...  38.2 us
    pallas_call x1, Pallas kernels, shards(): pl.pallas_call(hand_out, out_shape=shapes, in_specs=[vmem] * 5, out_specs...  1.01 us

profile of v3, /device:TPU:24, one launch (start us, length us, event | category | flops | bytes accessed | tf_op | source)
XLA Modules:
  0.0 39.8 jit_solution(15894494537261136920)
XLA Ops:
  0.6 38.2 %shard_map.101 = (bf16[256,512]{1,0:T(8,128)(2,1)S(1)}, bf16[256,512]{1,0:T(8,128)(2,1)S(1)}, bf16[256,512]{1,0:T(8,128)(2,1)S(1)}, bf16[256,512]{1,0:T(8,128)(2,1)S(1)}, f32[1,512]{1,0:T(1,128)S(1)}) custom-call(s32[1,4]{1,0:T(1,128)} %off_hbm.1, f32[1,512]{1,0:T(1,128)} %bitcast.14, bf16[256,512]{1,0:T(8,128)(2,1)} %bitcast.10, bf16[256,512]{1,0:T(8,128)(2,1)} %bitcast.11, ...), custom_call_target="tpu_custom_call" | custom-call | tf_op jit(solution)/shard_map/pallas_call | solution.py:393
  38.8 1.0 %shard_map.102 = (bf16[256,512]{1,0:T(8,128)(2,1)}, bf16[256,512]{1,0:T(8,128)(2,1)}, bf16[256,512]{1,0:T(8,128)(2,1)}, bf16[256,512]{1,0:T(8,128)(2,1)}, f32[1,512]{1,0:T(1,128)}) custom-call(bf16[256,512]{1,0:T(8,128)(2,1)S(1)} %get-tuple-element.15.refs_0_, bf16[256,512]{1,0:T(8,128)(2,1)S(1)} %get-tuple-element.16.refs_1_, ...), custom_call_target="tpu_custom_call" | custom-call | tf_op jit(solution)/shard_map/pallas_call | solution.py:421

commit v4 on v3

--- a/solution.py
+++ b/solution.py
@@ -11,7 +11,7 @@
 BLK = 64
 CH = 2048
 EPS = 1e-05
-CUTS = 2
+CUTS = 4
 
 MESH = pl.DeviceIdType.MESH
 F32 = jnp.float32
@@ -184,28 +184,42 @@
         sq_ref[...] = sq_ref[...] + attended * attended
         raw_ref[...] = raw_ref[...] + gain_ref[:, cols(h)] * g_ref[:, cols(h)].astype(F32) * attended
 
-    def staggered(ahead, local, relay, finish):
+    def staggered(ahead, local, relay, finish, passed_on):
         def before(h, carry):
             local(h)
             return carry
 
         lax.fori_loop(0, ahead, before, 0)
 
-        def step(h):
-            relay(h, 0)
-
-            @pl.when(h + ahead < heads)
-            def _():
-                local(h + ahead)
-
-            for part in range(1, CUTS):
-                relay(h, part)
-            finish(h)
-
-        each_head(step)
-
-    ahead = jnp.where(first | last, heads, jnp.minimum(place, heads))
-    staggered(ahead, attend, relay_right, add_carried)
+        @pl.when(first | last)
+        def _():
+            def step(h):
+                for part in range(CUTS):
+                    relay(h, part)
+                finish(h)
+
+            each_head(step)
+
+        @pl.when(jnp.logical_not(first | last))
+        def _():
+            def step(h):
+                for part in range(CUTS):
+                    relay(h, part)
+
+            each_head(step)
+            passed_on()
+
+            def rest(h):
+                @pl.when(h >= ahead)
+                def _():
+                    local(h)
+
+                finish(h)
+
+            each_head(rest)
+
+    ahead = jnp.where(first | last | (place > 1), heads, 1)
+    staggered(ahead, attend, relay_right, add_carried, lambda: None)
 
     stats[ten, 0:1, :] = jnp.sum(sq_ref[...].T, axis=0, keepdims=True)
     stats[ten, 1:2, :] = jnp.sum(raw_ref[...].T, axis=0, keepdims=True)
@@ -253,13 +267,13 @@
     for h in range(heads):
         after_norm(h)
 
+    gain_right = pltpu.make_async_remote_copy(
+        src_ref=gain_own, dst_ref=gain_come, send_sem=right_sem.at[0], recv_sem=right_sem.at[1],
+        device_id={"seq": place + 1}, device_id_type=MESH,
+    )
     gain_left = pltpu.make_async_remote_copy(
-        src_ref=gain_own, dst_ref=gain_come, send_sem=left_sem.at[0], recv_sem=left_sem.at[1],
+        src_ref=gain_all, dst_ref=gain_all, send_sem=left_sem.at[0], recv_sem=left_sem.at[1],
         device_id={"seq": place - 1}, device_id_type=MESH,
-    )
-    gain_right = pltpu.make_async_remote_copy(
-        src_ref=gain_all, dst_ref=gain_all, send_sem=right_sem.at[0], recv_sem=right_sem.at[1],
-        device_id={"seq": place + 1}, device_id_type=MESH,
     )
 
     def across(turn, slot):
@@ -269,45 +283,38 @@
             device_id={"dp": lax.rem(mine + turn, n_dp)}, device_id_type=MESH,
         )
 
-    def gain_relay():
+    def hand_gain_on():
         @pl.when(jnp.logical_not(last))
         def _():
             gain_left.wait_recv()
-            gain_own[...] = gain_own[...] + gain_come[...]
 
         @pl.when(jnp.logical_not(first))
         def _():
             gain_left.start()
 
-        @pl.when(first)
-        def _():
-            gain_dp[mine] = gain_own[...]
-            for turn in range(1, n_dp):
-                across(turn, mine).start()
-
-    def gain_total():
-        @pl.when(first)
-        def _():
-            for turn in range(1, n_dp):
-                across(turn, lax.rem(mine + turn, n_dp)).wait_recv()
-            total = gain_dp[0]
-            for i in range(1, n_dp):
-                total = total + gain_dp[i]
-            gain_all[...] = total
-
-        @pl.when(jnp.logical_not(first))
-        def _():
-            gain_right.wait_recv()
-
-        @pl.when(jnp.logical_not(last))
-        def _():
-            gain_right.start()
-
         gg_ref[...] = gain_all[...]
 
+    @pl.when(jnp.logical_not(first))
+    def _():
+        gain_right.wait_recv()
+        gain_own[...] = gain_own[...] + gain_come[...]
+
+    @pl.when(jnp.logical_not(last))
+    def _():
+        gain_right.start()
+
     @pl.when(last)
     def _():
-        gain_relay()
+        gain_dp[mine] = gain_own[...]
+        for turn in range(1, n_dp):
+            across(turn, mine).start()
+        for turn in range(1, n_dp):
+            across(turn, lax.rem(mine + turn, n_dp)).wait_recv()
+        total = gain_dp[0]
+        for i in range(1, n_dp):
+            total = total + gain_dp[i]
+        gain_all[...] = total
+        hand_gain_on()
 
     def relay_left(h, part):
         @pl.when(jnp.logical_not(last))
@@ -336,15 +343,14 @@
         gv = pv_ref[:, cols(h)] + dot(k_ref[:, cols(h)] * tail_ref[...], later, 1, 0)
         gv_ref[:, cols(h)] = gv.astype(BF16)
 
-        @pl.when((h == jnp.where(first, heads - 2, heads // 2 - 1)) & jnp.logical_not(last))
-        def _():
-            gain_relay()
-
     ahead = jnp.where(last, heads, jnp.minimum(n_seq - place, heads))
-    staggered(ahead, local_grads, relay_left, finish)
-    gain_total()
-
-    @pl.when(first)
+    staggered(ahead, local_grads, relay_left, finish, hand_gain_on)
+
+    @pl.when(first & (n_seq > 1))
+    def _():
+        hand_gain_on()
+
+    @pl.when(last)
     def _():
         for turn in range(1, n_dp):
             across(turn, mine).wait_send()

time: 40 us -> 33.9 us (0.85)
  the two profiles are of different devices: /device:TPU:24 before, /device:TPU:0 now
where the time goes in v4:
time: 33.9 us; the launch traced here: 33.8 us
  Pallas kernels  33.1 us (98%)
  between operations  0.64 us (2%)
    pallas_call x1, Pallas kernels, shards(): pl.pallas_call(functools.partial(kernel, sizes), out_shape=tuple((pltpu.V...  32.1 us
    pallas_call x1, Pallas kernels, shards(): pl.pallas_call(hand_out, out_shape=shapes, in_specs=[vmem] * 5, out_specs...  1.01 us

profile of v4, /device:TPU:0, one launch (start us, length us, event | category | flops | bytes accessed | tf_op | source)
XLA Modules:
  0.0 33.8 jit_solution(16401940289483364942)
XLA Ops:
  0.6 32.1 %shard_map.101 = (bf16[256,512]{1,0:T(8,128)(2,1)S(1)}, bf16[256,512]{1,0:T(8,128)(2,1)S(1)}, bf16[256,512]{1,0:T(8,128)(2,1)S(1)}, bf16[256,512]{1,0:T(8,128)(2,1)S(1)}, f32[1,512]{1,0:T(1,128)S(1)}) custom-call(s32[1,4]{1,0:T(1,128)} %off_hbm.1, f32[1,512]{1,0:T(1,128)} %bitcast.14, bf16[256,512]{1,0:T(8,128)(2,1)} %bitcast.10, bf16[256,512]{1,0:T(8,128)(2,1)} %bitcast.11, ...), custom_call_target="tpu_custom_call" | custom-call | tf_op jit(solution)/shard_map/pallas_call | solution.py:399
  32.7 1.0 %shard_map.102 = (bf16[256,512]{1,0:T(8,128)(2,1)}, bf16[256,512]{1,0:T(8,128)(2,1)}, bf16[256,512]{1,0:T(8,128)(2,1)}, bf16[256,512]{1,0:T(8,128)(2,1)}, f32[1,512]{1,0:T(1,128)}) custom-call(bf16[256,512]{1,0:T(8,128)(2,1)S(1)} %get-tuple-element.15.refs_0_, bf16[256,512]{1,0:T(8,128)(2,1)S(1)} %get-tuple-element.16.refs_1_, ...), custom_call_target="tpu_custom_call" | custom-call | tf_op jit(solution)/shard_map/pallas_call | solution.py:427

commit v5 on v4

--- a/solution.py
+++ b/solution.py
@@ -218,7 +218,7 @@
 
             each_head(rest)
 
-    ahead = jnp.where(first | last | (place > 1), heads, 1)
+    ahead = jnp.where(first | last, heads, jnp.minimum(2 * place - 1, heads))
     staggered(ahead, attend, relay_right, add_carried, lambda: None)
 
     stats[ten, 0:1, :] = jnp.sum(sq_ref[...].T, axis=0, keepdims=True)
@@ -343,7 +343,7 @@
         gv = pv_ref[:, cols(h)] + dot(k_ref[:, cols(h)] * tail_ref[...], later, 1, 0)
         gv_ref[:, cols(h)] = gv.astype(BF16)
 
-    ahead = jnp.where(last, heads, jnp.minimum(n_seq - place, heads))
+    ahead = jnp.where(first | last, heads, jnp.minimum(n_seq - 1 - place, heads))
     staggered(ahead, local_grads, relay_left, finish, hand_gain_on)
 
     @pl.when(first & (n_seq > 1))

time: 33.9 us -> 33.9 us (level)
  no operation moved by 1% of the time
where the time goes in v5:
time: 33.9 us; the launch traced here: 33.8 us
  Pallas kernels  33.1 us (98%)
  between operations  0.64 us (2%)
    pallas_call x1, Pallas kernels, shards(): pl.pallas_call(functools.partial(kernel, sizes), out_shape=tuple((pltpu.V...  32.1 us
    pallas_call x1, Pallas kernels, shards(): pl.pallas_call(hand_out, out_shape=shapes, in_specs=[vmem] * 5, out_specs...  1.01 us

profile of v5, /device:TPU:0, one launch (start us, length us, event | category | flops | bytes accessed | tf_op | source)
XLA Modules:
  0.0 33.8 jit_solution(1776567350468969089)
XLA Ops:
  0.6 32.1 %shard_map.101 = (bf16[256,512]{1,0:T(8,128)(2,1)S(1)}, bf16[256,512]{1,0:T(8,128)(2,1)S(1)}, bf16[256,512]{1,0:T(8,128)(2,1)S(1)}, bf16[256,512]{1,0:T(8,128)(2,1)S(1)}, f32[1,512]{1,0:T(1,128)S(1)}) custom-call(s32[1,4]{1,0:T(1,128)} %off_hbm.1, f32[1,512]{1,0:T(1,128)} %bitcast.14, bf16[256,512]{1,0:T(8,128)(2,1)} %bitcast.10, bf16[256,512]{1,0:T(8,128)(2,1)} %bitcast.11, ...), custom_call_target="tpu_custom_call" | custom-call | tf_op jit(solution)/shard_map/pallas_call | solution.py:399
  32.7 1.0 %shard_map.102 = (bf16[256,512]{1,0:T(8,128)(2,1)}, bf16[256,512]{1,0:T(8,128)(2,1)}, bf16[256,512]{1,0:T(8,128)(2,1)}, bf16[256,512]{1,0:T(8,128)(2,1)}, f32[1,512]{1,0:T(1,128)}) custom-call(bf16[256,512]{1,0:T(8,128)(2,1)S(1)} %get-tuple-element.15.refs_0_, bf16[256,512]{1,0:T(8,128)(2,1)S(1)} %get-tuple-element.16.refs_1_, ...), custom_call_target="tpu_custom_call" | custom-call | tf_op jit(solution)/shard_map/pallas_call | solution.py:427

commit v6 on v5

--- a/solution.py
+++ b/solution.py
@@ -13,6 +13,8 @@
 EPS = 1e-05
 CUTS = 4
 
+SKIP = 1
+
 MESH = pl.DeviceIdType.MESH
 F32 = jnp.float32
 BF16 = jnp.bfloat16
@@ -28,7 +30,9 @@
     off_ref, gain_ref, q_ref, k_ref, v_ref, g_ref,
     allow_ref, head_ref, tail_ref, wts_ref, att_ref, pre_ref, pk_ref, pv_ref, sq_ref, raw_ref,
     fsend, frecv, bsend, brecv, stats, gain_own, gain_come, gain_dp, gain_all,
+    ffar, bfar, flag, flag_left, flag_right,
     in_sem, fs_sem, fr_sem, bs_sem, br_sem, ss_sem, sr_sem, left_sem, dp_sem, right_sem,
+    ffs_sem, ffr_sem, bfs_sem, bfr_sem, flag_sem,
 ):
     n_dp, n_seq, n_ten = sizes
     length, width = q_ref.shape
@@ -38,6 +42,11 @@
     ten = lax.axis_index("tensor")
     mine = lax.axis_index("dp")
     first, last = place == 0, place == n_seq - 1
+    back = n_seq - 1 - place
+    hub, back_hub = lax.rem(place, 2) == 1, lax.rem(back, 2) == 1
+    far_out, far_in = hub & (back >= 2), hub & (place >= 3)
+    back_far_out, back_far_in = back_hub & (place >= 2), back_hub & (back >= 3)
+    near = heads - SKIP
 
     loads = [
         pltpu.make_async_copy(src, dst, in_sem.at[i])
@@ -68,7 +77,17 @@
         greet({"tensor": lax.rem(ten + turn, n_ten)})
     for turn in range(1, n_dp):
         greet({"dp": lax.rem(mine + turn, n_dp)})
+
+    @pl.when(far_in)
+    def _():
+        greet({"seq": place - 2})
+
+    @pl.when(back_far_in)
+    def _():
+        greet({"seq": place + 2})
+
     greeted = n_ten - 1 + n_dp - 1 + jnp.where(last, 0, 1) + jnp.where(first, 0, 1)
+    greeted = greeted + jnp.where(far_out, 1, 0) + jnp.where(back_far_out, 1, 0)
 
     def cols(h):
         return pl.ds(h * DH if isinstance(h, int) else pl.multiple_of(h * DH, DH), DH)
@@ -90,12 +109,40 @@
             device_id={"seq": place - 1}, device_id_type=MESH,
         )
 
-    def each_head(body):
+    def forward_far(h, part):
+        return pltpu.make_async_remote_copy(
+            src_ref=fsend.at[h, piece(part)], dst_ref=ffar.at[h - near, piece(part)],
+            send_sem=ffs_sem.at[h - near, part], recv_sem=ffr_sem.at[h - near, part],
+            device_id={"seq": place + 2}, device_id_type=MESH,
+        )
+
+    def backward_far(h, part):
+        return pltpu.make_async_remote_copy(
+            src_ref=bsend.at[h, piece(part)], dst_ref=bfar.at[h - near, piece(part)],
+            send_sem=bfs_sem.at[h - near, part], recv_sem=bfr_sem.at[h - near, part],
+            device_id={"seq": place - 2}, device_id_type=MESH,
+        )
+
+    flag_to_right = pltpu.make_async_remote_copy(
+        src_ref=flag, dst_ref=flag_left, send_sem=flag_sem.at[0], recv_sem=flag_sem.at[1],
+        device_id={"seq": place + 1}, device_id_type=MESH,
+    )
+    flag_to_left = pltpu.make_async_remote_copy(
+        src_ref=flag, dst_ref=flag_right, send_sem=flag_sem.at[2], recv_sem=flag_sem.at[3],
+        device_id={"seq": place - 1}, device_id_type=MESH,
+    )
+
+    def each_head(body, count=heads):
         def step(h, carry):
             body(h)
             return carry
 
-        lax.fori_loop(0, heads, step, 0)
+        lax.fori_loop(0, count, step, 0)
+
+    def each_head_apart(body):
+        each_head(body, near)
+        for h in range(near, heads):
+            body(h)
 
     loads[0].wait()
     starts_at = []
@@ -134,6 +181,15 @@
     tail(0)
     pl.semaphore_wait(barrier, greeted)
     launch(0)
+    flag[...] = jnp.where(jnp.full(flag.shape, starts, jnp.int32) == 0, 1.0, 0.0)
+
+    @pl.when(jnp.logical_not(last))
+    def _():
+        flag_to_right.start()
+
+    @pl.when(jnp.logical_not(first))
+    def _():
+        flag_to_left.start()
 
     def tails(h, carry):
         tail(h)
@@ -141,6 +197,15 @@
         return carry
 
     lax.fori_loop(1, heads, tails, 0)
+
+    @pl.when(jnp.logical_not(first | last | hub))
+    def _():
+        for h in range(near, heads):
+            for part in range(CUTS):
+                forward(h, part).start()
+
+    def joined(own, come, flags):
+        return own + jnp.where(jnp.broadcast_to(flags[0:1, :], come.shape) > 0, come, 0.0)
 
     rows_at = lax.broadcasted_iota(jnp.int32, (length, length), 0)
     cols_at = lax.broadcasted_iota(jnp.int32, (length, length), 1)
@@ -162,6 +227,10 @@
         load.wait()
 
     def relay_right(h, part):
+        if isinstance(h, int):
+            far_right(h, part)
+            return
+
         @pl.when(jnp.logical_not(first))
         def _():
             forward(h, part).wait_recv()
@@ -171,6 +240,34 @@
                 fsend[h, piece(part)] = passed(fsend[h, piece(part)], frecv[h, piece(part)])
                 forward(h, part).start()
 
+    def far_right(h, part):
+        at = piece(part)
+
+        @pl.when(jnp.logical_not(first))
+        def _():
+            if h == near and part == 0:
+                flag_to_right.wait_recv()
+            forward(h, part).wait_recv()
+
+        @pl.when(far_in)
+        def _():
+            forward_far(h, part).wait_recv()
+            frecv[h, at] = joined(frecv[h, at], ffar[h - near, at], flag_left)
+
+        @pl.when(hub & jnp.logical_not(last))
+        def _():
+            fsend[h, at] = passed(fsend[h, at], frecv[h, at])
+
+        @pl.when(far_out)
+        def _():
+            forward_far(h, part).start()
+
+        if part == CUTS - 1:
+            @pl.when(hub & jnp.logical_not(last))
+            def _():
+                for piece_at in range(CUTS):
+                    forward(h, piece_at).start()
+
     def attend(h):
         scores = dot(q_ref[:, cols(h)], k_ref[:, cols(h)], 1, 1)
         wts_ref[h] = (scores * allow_ref[...]).astype(BF16)
@@ -198,7 +295,7 @@
                     relay(h, part)
                 finish(h)
 
-            each_head(step)
+            each_head_apart(step)
 
         @pl.when(jnp.logical_not(first | last))
         def _():
@@ -206,7 +303,7 @@
                 for part in range(CUTS):
                     relay(h, part)
 
-            each_head(step)
+            each_head_apart(step)
             passed_on()
 
             def rest(h):
@@ -257,6 +354,12 @@
 
     each_head(before_norm)
 
+    @pl.when(jnp.logical_not(first | last | back_hub))
+    def _():
+        for h in range(near, heads):
+            for part in range(CUTS):
+                backward(h, part).start()
+
     def after_norm(h):
         normed = att_ref[:, cols(h)] * sq_ref[...]
         out_ref[:, cols(h)] = (gain_ref[:, cols(h)] * normed).astype(BF16)
@@ -317,6 +420,10 @@
         hand_gain_on()
 
     def relay_left(h, part):
+        if isinstance(h, int):
+            far_left(h, part)
+            return
+
         @pl.when(jnp.logical_not(last))
         def _():
             backward(h, part).wait_recv()
@@ -325,6 +432,34 @@
             def _():
                 bsend[h, piece(part)] = passed(bsend[h, piece(part)], brecv[h, piece(part)])
                 backward(h, part).start()
+
+    def far_left(h, part):
+        at = piece(part)
+
+        @pl.when(jnp.logical_not(last))
+        def _():
+            if h == near and part == 0:
+                flag_to_left.wait_recv()
+            backward(h, part).wait_recv()
+
+        @pl.when(back_far_in)
+        def _():
+            backward_far(h, part).wait_recv()
+            brecv[h, at] = joined(brecv[h, at], bfar[h - near, at], flag_right)
+
+        @pl.when(back_hub & jnp.logical_not(first))
+        def _():
+            bsend[h, at] = passed(bsend[h, at], brecv[h, at])
+
+        @pl.when(back_far_out)
+        def _():
+            backward_far(h, part).start()
+
+        if part == CUTS - 1:
+            @pl.when(back_hub & jnp.logical_not(first))
+            def _():
+                for piece_at in range(CUTS):
+                    backward(h, piece_at).start()
 
     def local_grads(h):
         pre = pre_ref[:, cols(h)]
@@ -364,6 +499,19 @@
             for part in range(CUTS):
                 forward(h, part).wait_send()
         gain_right.wait_send()
+        flag_to_right.wait_send()
+
+    @pl.when(far_out)
+    def _():
+        for h in range(near, heads):
+            for part in range(CUTS):
+                forward_far(h, part).wait_send()
+
+    @pl.when(back_far_out)
+    def _():
+        for h in range(near, heads):
+            for part in range(CUTS):
+                backward_far(h, part).wait_send()
 
     @pl.when(jnp.logical_not(first))
     def _():
@@ -371,6 +519,7 @@
             for part in range(CUTS):
                 backward(h, part).wait_send()
         gain_left.wait_send()
+        flag_to_left.wait_send()
 
 
 def hand_out(*refs):
@@ -418,8 +567,12 @@
             + [pltpu.VMEM((heads, DH, DH), F32)] * 4
             + [pltpu.VMEM((sizes[2], 2, length), F32), pltpu.VMEM((1, width), F32), pltpu.VMEM((1, width), F32)]
             + [pltpu.VMEM((sizes[0], 1, width), F32), pltpu.VMEM((1, width), F32)]
+            + [pltpu.VMEM((SKIP, DH, DH), F32)] * 2
+            + [pltpu.VMEM((8, DH), F32)] * 3
             + [dma((6,))] + [dma((heads, CUTS))] * 4
-            + [dma((sizes[2],)), dma((sizes[2],)), dma((2,)), dma((2, sizes[0])), dma((2,))],
+            + [dma((sizes[2],)), dma((sizes[2],)), dma((2,)), dma((2, sizes[0])), dma((2,))]
+            + [dma((SKIP, CUTS))] * 4
+            + [dma((4,))],
             compiler_params=pltpu.CompilerParams(
                 collective_id=0, has_side_effects=True, vmem_limit_bytes=61 * 1024 * 1024
             ),

time: 33.9 us -> 34.8 us (1.027)
  Pallas kernels: 33.1 us -> 34 us
    pallas_call x1, Pallas kernels: 32.1 us -> 33 us  [shards(): pl.pallas_call(functools.partial(kernel, sizes), out_shape=tuple((pltpu.V...]
where the time goes in v6:
time: 34.8 us; the launch traced here: 34.6 us
  Pallas kernels  34 us (98%)
  between operations  0.64 us (2%)
    pallas_call x1, Pallas kernels, shards(): pl.pallas_call(functools.partial(kernel, sizes), out_shape=tuple((pltpu.V...  33 us
    pallas_call x1, Pallas kernels, shards(): pl.pallas_call(hand_out, out_shape=shapes, in_specs=[vmem] * 5, out_specs...  1.01 us

profile of v6, /device:TPU:0, one launch (start us, length us, event | category | flops | bytes accessed | tf_op | source)
XLA Modules:
  0.0 34.6 jit_solution(16837263145788881036)
XLA Ops:
  0.6 33.0 %shard_map.101 = (bf16[256,512]{1,0:T(8,128)(2,1)S(1)}, bf16[256,512]{1,0:T(8,128)(2,1)S(1)}, bf16[256,512]{1,0:T(8,128)(2,1)S(1)}, bf16[256,512]{1,0:T(8,128)(2,1)S(1)}, f32[1,512]{1,0:T(1,128)S(1)}) custom-call(s32[1,4]{1,0:T(1,128)} %off_hbm.1, f32[1,512]{1,0:T(1,128)} %bitcast.14, bf16[256,512]{1,0:T(8,128)(2,1)} %bitcast.10, bf16[256,512]{1,0:T(8,128)(2,1)} %bitcast.11, ...), custom_call_target="tpu_custom_call" | custom-call | tf_op jit(solution)/shard_map/pallas_call | solution.py:548
  33.6 1.0 %shard_map.102 = (bf16[256,512]{1,0:T(8,128)(2,1)}, bf16[256,512]{1,0:T(8,128)(2,1)}, bf16[256,512]{1,0:T(8,128)(2,1)}, bf16[256,512]{1,0:T(8,128)(2,1)}, f32[1,512]{1,0:T(1,128)}) custom-call(bf16[256,512]{1,0:T(8,128)(2,1)S(1)} %get-tuple-element.15.refs_0_, bf16[256,512]{1,0:T(8,128)(2,1)S(1)} %get-tuple-element.16.refs_1_, ...), custom_call_target="tpu_custom_call" | custom-call | tf_op jit(solution)/shard_map/pallas_call | solution.py:580

commit v7 on v5

--- a/solution.py
+++ b/solution.py
@@ -28,7 +28,7 @@
     off_ref, gain_ref, q_ref, k_ref, v_ref, g_ref,
     allow_ref, head_ref, tail_ref, wts_ref, att_ref, pre_ref, pk_ref, pv_ref, sq_ref, raw_ref,
     fsend, frecv, bsend, brecv, stats, gain_own, gain_come, gain_dp, gain_all,
-    in_sem, fs_sem, fr_sem, bs_sem, br_sem, ss_sem, sr_sem, left_sem, dp_sem, right_sem,
+    in_sem, fs_sem, fr_sem, bs_sem, br_sem, ss_sem, sr_sem, left_sem, dp_sem, right_sem, turn_sem,
 ):
     n_dp, n_seq, n_ten = sizes
     length, width = q_ref.shape
@@ -125,8 +125,11 @@
     def tail(h):
         fsend[h] = dot(k_ref[:, cols(h)] * tail_ref[...], v_ref[:, cols(h)], 0, 0)
 
+    leads = first & (mine < n_dp - 1) & (n_seq > 1)
+    follows = first & (mine > 0) & (n_seq > 1)
+
     def launch(h):
-        @pl.when(first & (n_seq > 1))
+        @pl.when(first & (mine == 0) & (n_seq > 1))
         def _():
             for part in range(CUTS):
                 forward(h, part).start()
@@ -141,6 +144,20 @@
         return carry
 
     lax.fori_loop(1, heads, tails, 0)
+
+    @pl.when(follows)
+    def _():
+        pl.semaphore_wait(turn_sem, 1)
+        for h in range(heads):
+            for part in range(CUTS):
+                forward(h, part).start()
+
+    @pl.when(leads)
+    def _():
+        for h in range(heads - 1):
+            for part in range(CUTS):
+                forward(h, part).wait_send()
+        pl.semaphore_signal(turn_sem, inc=1, device_id={"dp": mine + 1}, device_id_type=MESH)
 
     rows_at = lax.broadcasted_iota(jnp.int32, (length, length), 0)
     cols_at = lax.broadcasted_iota(jnp.int32, (length, length), 1)
@@ -360,9 +377,14 @@
 
     @pl.when(jnp.logical_not(last))
     def _():
-        for h in range(heads):
-            for part in range(CUTS):
-                forward(h, part).wait_send()
+        @pl.when(jnp.logical_not(leads))
+        def _():
+            for h in range(heads - 1):
+                for part in range(CUTS):
+                    forward(h, part).wait_send()
+
+        for part in range(CUTS):
+            forward(heads - 1, part).wait_send()
         gain_right.wait_send()
 
     @pl.when(jnp.logical_not(first))
@@ -419,7 +441,8 @@
             + [pltpu.VMEM((sizes[2], 2, length), F32), pltpu.VMEM((1, width), F32), pltpu.VMEM((1, width), F32)]
             + [pltpu.VMEM((sizes[0], 1, width), F32), pltpu.VMEM((1, width), F32)]
             + [dma((6,))] + [dma((heads, CUTS))] * 4
-            + [dma((sizes[2],)), dma((sizes[2],)), dma((2,)), dma((2, sizes[0])), dma((2,))],
+            + [dma((sizes[2],)), dma((sizes[2],)), dma((2,)), dma((2, sizes[0])), dma((2,))]
+            + [pltpu.SemaphoreType.REGULAR],
             compiler_params=pltpu.CompilerParams(
                 collective_id=0, has_side_effects=True, vmem_limit_bytes=61 * 1024 * 1024
             ),

time: 33.9 us -> 36.1 us (1.065)
  Pallas kernels: 33.1 us -> 35.3 us
    pallas_call x1, Pallas kernels: 32.1 us -> 34.3 us  [shards(): pl.pallas_call(functools.partial(kernel, sizes), out_shape=tuple((pltpu.V...]
where the time goes in v7:
time: 36.1 us; the launch traced here: 36 us
  Pallas kernels  35.3 us (98%)
  between operations  0.64 us (2%)
    pallas_call x1, Pallas kernels, shards(): pl.pallas_call(functools.partial(kernel, sizes), out_shape=tuple((pltpu.V...  34.3 us
    pallas_call x1, Pallas kernels, shards(): pl.pallas_call(hand_out, out_shape=shapes, in_specs=[vmem] * 5, out_specs...  1.01 us

profile of v7, /device:TPU:0, one launch (start us, length us, event | category | flops | bytes accessed | tf_op | source)
XLA Modules:
  0.0 36.0 jit_solution(1657961133611769150)
XLA Ops:
  0.6 34.3 %shard_map.101 = (bf16[256,512]{1,0:T(8,128)(2,1)S(1)}, bf16[256,512]{1,0:T(8,128)(2,1)S(1)}, bf16[256,512]{1,0:T(8,128)(2,1)S(1)}, bf16[256,512]{1,0:T(8,128)(2,1)S(1)}, f32[1,512]{1,0:T(1,128)S(1)}) custom-call(s32[1,4]{1,0:T(1,128)} %off_hbm.1, f32[1,512]{1,0:T(1,128)} %bitcast.14, bf16[256,512]{1,0:T(8,128)(2,1)} %bitcast.10, bf16[256,512]{1,0:T(8,128)(2,1)} %bitcast.11, ...), custom_call_target="tpu_custom_call" | custom-call | tf_op jit(solution)/shard_map/pallas_call | solution.py:421
  35.0 1.0 %shard_map.102 = (bf16[256,512]{1,0:T(8,128)(2,1)}, bf16[256,512]{1,0:T(8,128)(2,1)}, bf16[256,512]{1,0:T(8,128)(2,1)}, bf16[256,512]{1,0:T(8,128)(2,1)}, f32[1,512]{1,0:T(1,128)}) custom-call(bf16[256,512]{1,0:T(8,128)(2,1)S(1)} %get-tuple-element.15.refs_0_, bf16[256,512]{1,0:T(8,128)(2,1)S(1)} %get-tuple-element.16.refs_1_, ...), custom_call_target="tpu_custom_call" | custom-call | tf_op jit(solution)/shard_map/pallas_call | solution.py:450

commit v8 on v5

--- a/solution.py
+++ b/solution.py
@@ -27,7 +27,7 @@
     out_ref, gq_ref, gk_ref, gv_ref, gg_ref,
     off_ref, gain_ref, q_ref, k_ref, v_ref, g_ref,
     allow_ref, head_ref, tail_ref, wts_ref, att_ref, pre_ref, pk_ref, pv_ref, sq_ref, raw_ref,
-    fsend, frecv, bsend, brecv, stats, gain_own, gain_come, gain_dp, gain_all,
+    fsend, frecv, bsend, brecv, stats, gain_own, gain_come, gain_dp,
     in_sem, fs_sem, fr_sem, bs_sem, br_sem, ss_sem, sr_sem, left_sem, dp_sem, right_sem,
 ):
     n_dp, n_seq, n_ten = sizes
@@ -38,6 +38,8 @@
     ten = lax.axis_index("tensor")
     mine = lax.axis_index("dp")
     first, last = place == 0, place == n_seq - 1
+    back = n_seq - 1 - place
+    group = n_dp * n_seq
 
     loads = [
         pltpu.make_async_copy(src, dst, in_sem.at[i])
@@ -68,7 +70,14 @@
         greet({"tensor": lax.rem(ten + turn, n_ten)})
     for turn in range(1, n_dp):
         greet({"dp": lax.rem(mine + turn, n_dp)})
+
+    for d in range(n_dp):
+        @pl.when((back > 1) | ((back == 1) & (mine != d)))
+        def _():
+            greet({"dp": d, "seq": n_seq - 1})
+
     greeted = n_ten - 1 + n_dp - 1 + jnp.where(last, 0, 1) + jnp.where(first, 0, 1)
+    greeted = greeted + jnp.where(last, n_dp * (n_seq - 1) - (1 if n_seq > 1 else 0), 0)
 
     def cols(h):
         return pl.ds(h * DH if isinstance(h, int) else pl.multiple_of(h * DH, DH), DH)
@@ -271,28 +280,20 @@
         src_ref=gain_own, dst_ref=gain_come, send_sem=right_sem.at[0], recv_sem=right_sem.at[1],
         device_id={"seq": place + 1}, device_id_type=MESH,
     )
-    gain_left = pltpu.make_async_remote_copy(
-        src_ref=gain_all, dst_ref=gain_all, send_sem=left_sem.at[0], recv_sem=left_sem.at[1],
-        device_id={"seq": place - 1}, device_id_type=MESH,
-    )
-
-    def across(turn, slot):
+    def gain_out(turn):
+        other = lax.rem(mine * n_seq + place + turn, group)
         return pltpu.make_async_remote_copy(
-            src_ref=gain_dp.at[slot], dst_ref=gain_dp.at[slot],
-            send_sem=dp_sem.at[0, turn], recv_sem=dp_sem.at[1, slot],
-            device_id={"dp": lax.rem(mine + turn, n_dp)}, device_id_type=MESH,
-        )
-
-    def hand_gain_on():
-        @pl.when(jnp.logical_not(last))
-        def _():
-            gain_left.wait_recv()
-
-        @pl.when(jnp.logical_not(first))
-        def _():
-            gain_left.start()
-
-        gg_ref[...] = gain_all[...]
+            src_ref=gain_dp.at[mine], dst_ref=gain_dp.at[mine],
+            send_sem=left_sem.at[turn], recv_sem=dp_sem.at[mine],
+            device_id={"dp": lax.div(other, n_seq), "seq": lax.rem(other, n_seq)}, device_id_type=MESH,
+        )
+
+    def gain_in(d):
+        return pltpu.make_async_remote_copy(
+            src_ref=gain_dp.at[d], dst_ref=gain_dp.at[d],
+            send_sem=left_sem.at[0], recv_sem=dp_sem.at[d],
+            device_id={"seq": 0}, device_id_type=MESH,
+        )
 
     @pl.when(jnp.logical_not(first))
     def _():
@@ -306,15 +307,12 @@
     @pl.when(last)
     def _():
         gain_dp[mine] = gain_own[...]
-        for turn in range(1, n_dp):
-            across(turn, mine).start()
-        for turn in range(1, n_dp):
-            across(turn, lax.rem(mine + turn, n_dp)).wait_recv()
-        total = gain_dp[0]
-        for i in range(1, n_dp):
-            total = total + gain_dp[i]
-        gain_all[...] = total
-        hand_gain_on()
+
+        def send(turn, carry):
+            gain_out(turn).start()
+            return carry
+
+        lax.fori_loop(1, group, send, 0)
 
     def relay_left(h, part):
         @pl.when(jnp.logical_not(last))
@@ -344,16 +342,25 @@
         gv_ref[:, cols(h)] = gv.astype(BF16)
 
     ahead = jnp.where(first | last, heads, jnp.minimum(n_seq - 1 - place, heads))
-    staggered(ahead, local_grads, relay_left, finish, hand_gain_on)
-
-    @pl.when(first & (n_seq > 1))
-    def _():
-        hand_gain_on()
+    staggered(ahead, local_grads, relay_left, finish, lambda: None)
+
+    for d in range(n_dp):
+        @pl.when(jnp.logical_not(last & (mine == d)))
+        def _():
+            gain_in(d).wait_recv()
+
+    total = gain_dp[0]
+    for d in range(1, n_dp):
+        total = total + gain_dp[d]
+    gg_ref[...] = total
 
     @pl.when(last)
     def _():
-        for turn in range(1, n_dp):
-            across(turn, mine).wait_send()
+        def sent(turn, carry):
+            gain_out(turn).wait_send()
+            return carry
+
+        lax.fori_loop(1, group, sent, 0)
 
     for turn in range(1, n_ten):
         exchange(turn, ten).wait_send()
@@ -370,7 +377,6 @@
         for h in range(heads):
             for part in range(CUTS):
                 backward(h, part).wait_send()
-        gain_left.wait_send()
 
 
 def hand_out(*refs):
@@ -417,9 +423,9 @@
             ]
             + [pltpu.VMEM((heads, DH, DH), F32)] * 4
             + [pltpu.VMEM((sizes[2], 2, length), F32), pltpu.VMEM((1, width), F32), pltpu.VMEM((1, width), F32)]
-            + [pltpu.VMEM((sizes[0], 1, width), F32), pltpu.VMEM((1, width), F32)]
+            + [pltpu.VMEM((sizes[0], 1, width), F32)]
             + [dma((6,))] + [dma((heads, CUTS))] * 4
-            + [dma((sizes[2],)), dma((sizes[2],)), dma((2,)), dma((2, sizes[0])), dma((2,))],
+            + [dma((sizes[2],)), dma((sizes[2],)), dma((sizes[0] * sizes[1],)), dma((sizes[0],)), dma((2,))],
             compiler_params=pltpu.CompilerParams(
                 collective_id=0, has_side_effects=True, vmem_limit_bytes=61 * 1024 * 1024
             ),

time: 33.9 us -> 34 us (level)
  no operation moved by 1% of the time
where the time goes in v8:
time: 34 us; the launch traced here: 33.9 us
  Pallas kernels  33.2 us (98%)
  between operations  0.64 us (2%)
    pallas_call x1, Pallas kernels, shards(): pl.pallas_call(functools.partial(kernel, sizes), out_shape=tuple((pltpu.V...  32.2 us
    pallas_call x1, Pallas kernels, shards(): pl.pallas_call(hand_out, out_shape=shapes, in_specs=[vmem] * 5, out_specs...  1.01 us

profile of v8, /device:TPU:0, one launch (start us, length us, event | category | flops | bytes accessed | tf_op | source)
XLA Modules:
  0.0 33.9 jit_solution(690350995447789507)
XLA Ops:
  0.6 32.2 %shard_map.101 = (bf16[256,512]{1,0:T(8,128)(2,1)S(1)}, bf16[256,512]{1,0:T(8,128)(2,1)S(1)}, bf16[256,512]{1,0:T(8,128)(2,1)S(1)}, bf16[256,512]{1,0:T(8,128)(2,1)S(1)}, f32[1,512]{1,0:T(1,128)S(1)}) custom-call(s32[1,4]{1,0:T(1,128)} %off_hbm.1, f32[1,512]{1,0:T(1,128)} %bitcast.14, bf16[256,512]{1,0:T(8,128)(2,1)} %bitcast.10, bf16[256,512]{1,0:T(8,128)(2,1)} %bitcast.11, ...), custom_call_target="tpu_custom_call" | custom-call | tf_op jit(solution)/shard_map/pallas_call | solution.py:405
  32.8 1.0 %shard_map.102 = (bf16[256,512]{1,0:T(8,128)(2,1)}, bf16[256,512]{1,0:T(8,128)(2,1)}, bf16[256,512]{1,0:T(8,128)(2,1)}, bf16[256,512]{1,0:T(8,128)(2,1)}, f32[1,512]{1,0:T(1,128)}) custom-call(bf16[256,512]{1,0:T(8,128)(2,1)S(1)} %get-tuple-element.15.refs_0_, bf16[256,512]{1,0:T(8,128)(2,1)S(1)} %get-tuple-element.16.refs_1_, ...), custom_call_target="tpu_custom_call" | custom-call | tf_op jit(solution)/shard_map/pallas_call | solution.py:433

commit v9 on v8

--- a/solution.py
+++ b/solution.py
@@ -28,7 +28,7 @@
     off_ref, gain_ref, q_ref, k_ref, v_ref, g_ref,
     allow_ref, head_ref, tail_ref, wts_ref, att_ref, pre_ref, pk_ref, pv_ref, sq_ref, raw_ref,
     fsend, frecv, bsend, brecv, stats, gain_own, gain_come, gain_dp,
-    in_sem, fs_sem, fr_sem, bs_sem, br_sem, ss_sem, sr_sem, left_sem, dp_sem, right_sem,
+    in_sem, fs_sem, fr_sem, bs_sem, br_sem, ss_sem, sr_sem, left_sem, dp_sem, right_sem, turn_sem,
 ):
     n_dp, n_seq, n_ten = sizes
     length, width = q_ref.shape
@@ -134,8 +134,11 @@
     def tail(h):
         fsend[h] = dot(k_ref[:, cols(h)] * tail_ref[...], v_ref[:, cols(h)], 0, 0)
 
+    leads = first & (mine < n_dp - 1) & (n_seq > 1)
+    follows = first & (mine > 0) & (n_seq > 1)
+
     def launch(h):
-        @pl.when(first & (n_seq > 1))
+        @pl.when(first & (mine == 0) & (n_seq > 1))
         def _():
             for part in range(CUTS):
                 forward(h, part).start()
@@ -150,6 +153,20 @@
         return carry
 
     lax.fori_loop(1, heads, tails, 0)
+
+    @pl.when(follows)
+    def _():
+        pl.semaphore_wait(turn_sem, 1)
+        for h in range(heads):
+            for part in range(CUTS):
+                forward(h, part).start()
+
+    @pl.when(leads)
+    def _():
+        for h in range(heads // 2):
+            for part in range(CUTS):
+                forward(h, part).wait_send()
+        pl.semaphore_signal(turn_sem, inc=1, device_id={"dp": mine + 1}, device_id_type=MESH)
 
     rows_at = lax.broadcasted_iota(jnp.int32, (length, length), 0)
     cols_at = lax.broadcasted_iota(jnp.int32, (length, length), 1)
@@ -367,7 +384,13 @@
 
     @pl.when(jnp.logical_not(last))
     def _():
-        for h in range(heads):
+        @pl.when(jnp.logical_not(leads))
+        def _():
+            for h in range(heads // 2):
+                for part in range(CUTS):
+                    forward(h, part).wait_send()
+
+        for h in range(heads // 2, heads):
             for part in range(CUTS):
                 forward(h, part).wait_send()
         gain_right.wait_send()
@@ -425,7 +448,8 @@
             + [pltpu.VMEM((sizes[2], 2, length), F32), pltpu.VMEM((1, width), F32), pltpu.VMEM((1, width), F32)]
             + [pltpu.VMEM((sizes[0], 1, width), F32)]
             + [dma((6,))] + [dma((heads, CUTS))] * 4
-            + [dma((sizes[2],)), dma((sizes[2],)), dma((sizes[0] * sizes[1],)), dma((sizes[0],)), dma((2,))],
+            + [dma((sizes[2],)), dma((sizes[2],)), dma((sizes[0] * sizes[1],)), dma((sizes[0],)), dma((2,))]
+            + [pltpu.SemaphoreType.REGULAR],
             compiler_params=pltpu.CompilerParams(
                 collective_id=0, has_side_effects=True, vmem_limit_bytes=61 * 1024 * 1024
             ),

time: 34 us -> 36.2 us (1.065)
  Pallas kernels: 33.2 us -> 35.4 us
    pallas_call x1, Pallas kernels: 32.2 us -> 34.4 us  [shards(): pl.pallas_call(functools.partial(kernel, sizes), out_shape=tuple((pltpu.V...]
where the time goes in v9:
time: 36.2 us; the launch traced here: 36.1 us
  Pallas kernels  35.4 us (98%)
  between operations  0.64 us (2%)
    pallas_call x1, Pallas kernels, shards(): pl.pallas_call(functools.partial(kernel, sizes), out_shape=tuple((pltpu.V...  34.4 us
    pallas_call x1, Pallas kernels, shards(): pl.pallas_call(hand_out, out_shape=shapes, in_specs=[vmem] * 5, out_specs...  1.01 us

profile of v9, /device:TPU:0, one launch (start us, length us, event | category | flops | bytes accessed | tf_op | source)
XLA Modules:
  0.0 36.1 jit_solution(15893214430077860538)
XLA Ops:
  0.6 34.4 %shard_map.101 = (bf16[256,512]{1,0:T(8,128)(2,1)S(1)}, bf16[256,512]{1,0:T(8,128)(2,1)S(1)}, bf16[256,512]{1,0:T(8,128)(2,1)S(1)}, bf16[256,512]{1,0:T(8,128)(2,1)S(1)}, f32[1,512]{1,0:T(1,128)S(1)}) custom-call(s32[1,4]{1,0:T(1,128)} %off_hbm.1, f32[1,512]{1,0:T(1,128)} %bitcast.14, bf16[256,512]{1,0:T(8,128)(2,1)} %bitcast.10, bf16[256,512]{1,0:T(8,128)(2,1)} %bitcast.11, ...), custom_call_target="tpu_custom_call" | custom-call | tf_op jit(solution)/shard_map/pallas_call | solution.py:428
  35.1 1.0 %shard_map.102 = (bf16[256,512]{1,0:T(8,128)(2,1)}, bf16[256,512]{1,0:T(8,128)(2,1)}, bf16[256,512]{1,0:T(8,128)(2,1)}, bf16[256,512]{1,0:T(8,128)(2,1)}, f32[1,512]{1,0:T(1,128)}) custom-call(bf16[256,512]{1,0:T(8,128)(2,1)S(1)} %get-tuple-element.15.refs_0_, bf16[256,512]{1,0:T(8,128)(2,1)S(1)} %get-tuple-element.16.refs_1_, ...), custom_call_target="tpu_custom_call" | custom-call | tf_op jit(solution)/shard_map/pallas_call | solution.py:457
